TPU v7x, 32 devices: a whole 2x2x4 slice. The times are simulated.
32 devices in a mesh: light: 4 (over z), view: 8 (over y, x, core).
Axes of the slice: x: 2, y: 2, z: 4, core: 2. Of those that a mesh axis runs over, the one named last changes fastest.
Arguments:
- density: bfloat16 [1024, 64, 512], P('view', None, 'light'), may hold values from 0 to 8, as said below
- color_coef: float32 [3, 4], replicated, may hold values from 0.2 to 1
Outputs:
- image: float32 [3, 64, 512], P(None, 'view', 'light')
Inputs may be any that keep to these rules, and one draw needn't show every extreme that they name: `density`: densities are nonnegative.
All inputs are finite; a program needn't handle non-finite values.
Results may differ from a plain program's by a relative error of at most 0.0003.
Values sent between devices are 32-bit elements; how exact they have to be, the bound alone decides.
No kernel may reach another device: no remote copies, remote signals or barrier semaphores. Data moves between devices by JAX's collectives and lax.ppermute only.
A program may use at most 64 MiB of HBM per device.

v0:
```python
import jax
import jax.numpy as jnp
from jax import lax
from jax.sharding import PartitionSpec as P


def shifted(x, axis, by):
    devices = lax.axis_size(axis)
    pairs = [(i, i + by) for i in range(devices) if 0 <= i + by < devices]
    return lax.ppermute(x, axis, pairs)


def composite(pieces):
    depths = pieces[:, 3]
    before = jnp.cumsum(depths, axis=0) - depths
    return jnp.sum(pieces[:, :3] * jnp.exp(-before)[:, None], axis=0)


def body(density, color_coef):
    values = density.astype(jnp.float32)
    view_cells = values.shape[0]
    planes = values.shape[1]
    light_cells = values.shape[2]
    light_count = lax.axis_size("light")
    view_count = lax.axis_size("view")
    total_light = light_cells * light_count
    total_view = view_cells * view_count
    light_step = 2.0 / total_light * values
    light_run = jnp.cumsum(light_step, axis=2)
    sheet_total = light_run[:, :, -1]
    view_step = 2.0 / total_view * values
    view_run = jnp.cumsum(view_step, axis=0)
    alpha = 1.0 - jnp.exp(-view_step)
    coef = color_coef[:, :, None, None, None]
    palette = coef[:, 0] + values[None] * (
        coef[:, 1] + values[None] * (coef[:, 2] + values[None] * coef[:, 3])
    )
    upstream = jnp.zeros_like(sheet_total)
    for hop_index in range(light_count - 1):
        upstream = shifted(upstream + sheet_total, "light", 1)
    lit = jnp.exp(-(upstream[:, :, None] + light_run - light_step))
    weight = alpha * (0.3 + lit) * jnp.exp(-(view_run - view_step))
    partial_value = jnp.sum(palette * weight[None], axis=1)
    depth_sheet = view_run[-1]
    row_count = planes // view_count
    stacked = jnp.concatenate([partial_value, depth_sheet[None]], axis=0)
    received = lax.all_to_all(stacked, "view", split_axis=1, concat_axis=0, tiled=True)
    picture = composite(received.reshape(view_count, 4, row_count, light_cells))
    return picture


def solution(mesh):
    placed = (P("view", None, "light"), P())
    return jax.shard_map(
        body, mesh=mesh, in_specs=placed, out_specs=P(None, "view", "light"), check_vma=False
    )
```

profile of v0, /device:TPU:0, one launch (start us, length us, event | category | flops | bytes accessed | tf_op | source)
XLA Modules:
  0.0 67.1 jit_solution(4534000382134850085)
XLA Ops:
  0.0 3.8 %copy.26 = bf16[128,64,128]{0,1,2:T(8,128)(2,1)S(1)} copy(bf16[128,64,128]{2,1,0:T(8,128)(2,1)} %param.2) | data formatting | bytes 4194304 | tf_op args[0]
  3.8 0.5 fusion
  4.3 2.0 %copy-done = f32[128,64,128]{0,1,2:T(8,128)} copy-done((f32[128,64,128]{0,1,2:T(8,128)}, f32[128,64,128]{0,1,2:T(8,128)S(1)}, u32[]{:S(2)}) %copy-start) | copy-done | bytes 4194328
  6.3 4.9 %collective-permute-start = (f32[128,64]{0,1:T(8,128)S(1)}, f32[128,64]{0,1:T(8,128)S(1)}, u32[]{:S(2)}, u32[]{:S(2)}) collective-permute-start(f32[128,64]{0,1:T(8,128)S(1)} %slice_bitcast_fusion), channel_id=1, source_target_pairs={{0,8},{8,16},{16,24},{1,9},{9,17},{17,25},{2,10},{10,18},{18,26},{... | collective-permute-start | bytes 98312 | tf_op jit(solution)/shard_map/ppermute | solution.py:10
  11.2 2.5 %convert_multiply_fusion = f32[128,64,128]{0,1,2:T(8,128)} fusion(bf16[128,64,128]{0,1,2:T(8,128)(2,1)S(1)} %copy.26), kind=kLoop, calls=%fused_computation.5 | loop fusion | flops 2097152 | bytes 6291456 | tf_op jit(solution)/shard_map/mul | solution.py:31
  13.7 5.5 %copy.28 = f32[128,64,128]{2,1,0:T(8,128)} copy(f32[128,64,128]{0,1,2:T(8,128)} %convert_multiply_fusion) | data formatting | bytes 8388608 | tf_op jit(solution)/shard_map/mul | solution.py:31
  19.2 0.0 collective-permute-done
  19.2 0.8 %fusion.10 = f32[128,64]{0,1:T(8,128)S(1)} fusion(f32[128,64]{0,1:T(8,128)S(1)} %collective-permute-done, f32[128,64,128]{0,1,2:T(8,128)} %copy-done), kind=kLoop, calls=%fused_computation.21 | loop fusion | flops 8192 | bytes 98304 | tf_op jit(solution)/shard_map/add | solution.py:40
  19.9 3.6 %collective-permute-start.1 = (f32[128,64]{0,1:T(8,128)S(1)}, f32[128,64]{0,1:T(8,128)S(1)}, u32[]{:S(2)}, u32[]{:S(2)}) collective-permute-start(f32[128,64]{0,1:T(8,128)S(1)} %fusion.10), channel_id=1, source_target_pairs={{0,8},{8,16},{16,24},{1,9},{9,17},{17,25},{2,10},{10,18},{18,26},{... | collective-permute-start | bytes 98312 | tf_op jit(solution)/shard_map/ppermute | solution.py:10
  23.6 2.5 %fusion.11 = f32[128,64,128]{2,1,0:T(8,128)S(1)} fusion(f32[128,64,128]{2,1,0:T(8,128)} %copy.28), kind=kOutput, calls=%fused_computation.22 | output fusion | flops 133169152 | bytes 8388608 | tf_op jit(solution)/shard_map/jit(cumsum)/reduce_window_sum | solution.py:32
  26.1 0.0 collective-permute-done.1
  26.1 0.8 %fusion.9 = f32[128,64]{0,1:T(8,128)S(1)} fusion(f32[128,64]{0,1:T(8,128)S(1)} %collective-permute-done.1, f32[128,64,128]{0,1,2:T(8,128)} %copy-done), kind=kLoop, calls=%fused_computation.20 | loop fusion | flops 8192 | bytes 98304 | tf_op jit(solution)/shard_map/add | solution.py:40
  26.9 3.5 %collective-permute-start.2 = (f32[128,64]{0,1:T(8,128)S(1)}, f32[128,64]{0,1:T(8,128)S(1)}, u32[]{:S(2)}, u32[]{:S(2)}) collective-permute-start(f32[128,64]{0,1:T(8,128)S(1)} %fusion.9), channel_id=1, source_target_pairs={{0,8},{8,16},{16,24},{1,9},{9,17},{17,25},{2,10},{10,18},{18,26},{... | collective-permute-start | bytes 98312 | tf_op jit(solution)/shard_map/ppermute | solution.py:10
  30.4 0.2 slice_reduce_fusion.3
  30.6 5.5 %copy.29 = f32[128,64,128]{0,1,2:T(8,128)} copy(f32[128,64,128]{2,1,0:T(8,128)} %copy-done.1) | data formatting | bytes 8388608 | tf_op jit(solution)/shard_map/jit(cumsum)/reduce_window_sum | solution.py:32
  36.1 3.6 %copy.27 = f32[128,64,128]{2,1,0:T(8,128)} copy(bf16[128,64,128]{0,1,2:T(8,128)(2,1)S(1)} %copy.26) | data formatting | bytes 6291456 | tf_op jit(solution)/shard_map/convert_element_type | solution.py:20
  39.8 0.0 collective-permute-done.2
  39.8 6.0 %exponential_multiply_fusion = f32[128,64,128]{0,1,2:T(8,128)} fusion(f32[128,64,128]{0,1,2:T(8,128)} %copy.29, f32[128,64,128]{0,1,2:T(8,128)} %copy-done, bf16[128,64,128]{0,1,2:T(8,128)(2,1)S(1)} %copy.26, f32[128,64]{0,1:T(8,128)S(1)} %collective-permute-done.2), kind=kLoop, calls=%fused_computation.1 | loop fusion | flops 13631488 | bytes 14712832 | tf_op jit(solution)/shard_map/mul | solution.py:42
  45.8 5.5 %copy.30 = f32[128,64,128]{2,1,0:T(8,128)} copy(f32[128,64,128]{0,1,2:T(8,128)} %exponential_multiply_fusion) | data formatting | bytes 8388608 | tf_op jit(solution)/shard_map/mul | solution.py:42
  51.3 5.9 %multiply_reduce_fusion = f32[3,64,128]{2,1,0:T(8,128)S(1)} fusion(f32[128,64,128]{2,1,0:T(8,128)} %copy.30, f32[3]{0:T(128)S(1)} %get-tuple-element.6, f32[3]{0:T(128)S(1)} %get-tuple-element.7, f32[3]{0:T(128)S(1)} %get-tuple-element.8, f32[128,64,128]{2,1,0:T(8,128)} %copy.27, f32[3]{0:T(128)S(1)} %get-tuple-element.5), kind=kLoop, calls=%fused_computation | loop fusion | flops 25141248 | bytes 8486960 | tf_op jit(solution)/shard_map/reduce_sum | solution.py:43
  57.2 0.1 copy.31
  57.3 9.1 %all_to_all.15 = f32[4,64,128]{2,0,1:T(4,128)S(1)} all-to-all(f32[4,64,128]{2,0,1:T(4,128)S(1)} %copy.31), channel_id=1, replica_groups=mesh['light'=4,'view'=8] {'view'}, dimensions={1} | all-to-all | bytes 262144 | tf_op jit(solution)/shard_map/all_to_all | solution.py:47
  66.4 0.1 fusion.5
  66.5 0.6 copy.32
  (10 shorter events, 0.1 us)
Async XLA Ops:
  4.3 2.0 %copy-start = (f32[128,64,128]{0,1,2:T(8,128)}, f32[128,64,128]{0,1,2:T(8,128)S(1)}, u32[]{:S(2)}) copy-start(f32[128,64,128]{0,1,2:T(8,128)S(1)} %fusion) | copy-start | bytes 12582916
  6.3 12.9 %collective-permute-start = (f32[128,64]{0,1:T(8,128)S(1)}, f32[128,64]{0,1:T(8,128)S(1)}, u32[]{:S(2)}, u32[]{:S(2)}) collective-permute-start(f32[128,64]{0,1:T(8,128)S(1)} %slice_bitcast_fusion), channel_id=1, source_target_pairs={{0,8},{8,16},{16,24},{1,9},{9,17},{17,25},{2,10},{10,18},{18,26},{... | collective-permute-start | bytes 98312 | tf_op jit(solution)/shard_map/ppermute | solution.py:10
  19.9 10.5 %copy-start.2 = (f32[3,4]{1,0:T(4,128)S(1)}, f32[3,4]{1,0:T(4,128)}, u32[]{:S(2)}) copy-start(f32[3,4]{1,0:T(4,128)} %param.3) | copy-start | bytes 148
  19.9 6.1 %collective-permute-start.1 = (f32[128,64]{0,1:T(8,128)S(1)}, f32[128,64]{0,1:T(8,128)S(1)}, u32[]{:S(2)}, u32[]{:S(2)}) collective-permute-start(f32[128,64]{0,1:T(8,128)S(1)} %fusion.10), channel_id=1, source_target_pairs={{0,8},{8,16},{16,24},{1,9},{9,17},{17,25},{2,10},{10,18},{18,26},{... | collective-permute-start | bytes 98312 | tf_op jit(solution)/shard_map/ppermute | solution.py:10
  26.1 4.5 %copy-start.1 = (f32[128,64,128]{2,1,0:T(8,128)}, f32[128,64,128]{2,1,0:T(8,128)S(1)}, u32[]{:S(2)}) copy-start(f32[128,64,128]{2,1,0:T(8,128)S(1)} %fusion.11) | copy-start | bytes 12582916
  26.9 12.8 %collective-permute-start.2 = (f32[128,64]{0,1:T(8,128)S(1)}, f32[128,64]{0,1:T(8,128)S(1)}, u32[]{:S(2)}, u32[]{:S(2)}) collective-permute-start(f32[128,64]{0,1:T(8,128)S(1)} %fusion.9), channel_id=1, source_target_pairs={{0,8},{8,16},{16,24},{1,9},{9,17},{17,25},{2,10},{10,18},{18,26},{... | collective-permute-start | bytes 98312 | tf_op jit(solution)/shard_map/ppermute | solution.py:10
  51.3 5.9 %slice-start = ((f32[128,64,128]{2,1,0:T(8,128)}), f32[1,64,128]{2,1,0:T(8,128)S(1)}, s32[]{:S(2)}) async-start(f32[128,64,128]{2,1,0:T(8,128)} %copy-done.1), calls=%async_computation.1 | async-start | bytes 65536 | tf_op jit(solution)/shard_map/slice | solution.py:44
where the time goes:
time: 67.8 us; the launch traced here: 67.1 us
  local copies, waits for them, and re-layouts  26.8 us (40%)
  other arithmetic  19.1 us (28%)
  starting transfers between devices  12 us (18%)
  blocking collectives  9.05 us (13%)
    ppermute x3, starting transfers between devices, shifted(): return lax.ppermute(x, axis, pairs)  12 us
    all_to_all x1, blocking collectives, body(): lax.all_to_all(stacked, 'view', split_axis=1, concat_axis=0, tiled=True)  9.05 us
    mul x1, other arithmetic, body(): weight = alpha * (0.3 + lit) * jnp.exp(-(view_run - view_step))  6.04 us
    reduce_sum x1, other arithmetic, body(): partial_value = jnp.sum(palette * weight[None], axis=1)  5.88 us
    unnamed x7, local copies, waits for them, and re-layouts  5.8 us
    another operation x1, local copies, waits for them, and re-layouts, body(): view_run = jnp.cumsum(view_step, axis=0)  5.49 us
    mul x1, local copies, waits for them, and re-layouts, body(): weight = alpha * (0.3 + lit) * jnp.exp(-(view_run - view_step))  5.47 us
    mul x1, local copies, waits for them, and re-layouts, body(): view_step = 2.0 / total_view * values  5.46 us
  transfers between devices with their start and end apart: 3, of which 0 were waited for; matrix products, arithmetic and copies ran while one was open for 30% of the time, Pallas kernels for 0%

commit v1 on v0

v1 whole, which is shorter than its diff:
```python
import functools
import math

import jax
import jax.numpy as jnp
from jax import lax
from jax.experimental import pallas as pl
from jax.experimental.pallas import tpu as pltpu
from jax.sharding import PartitionSpec as P

VMEM = pltpu.VMEM
LOG2E = math.log2(math.e)
STEP = 8


def swapped(x, axis, mask):
    devices = lax.axis_size(axis)
    return lax.ppermute(x, axis, [(i, i ^ mask) for i in range(devices)])


def paired(x, rows):
    half = x.shape[0] // 2
    lanes = x.shape[-1]
    return jnp.concatenate(
        [x[:half].reshape(half * rows, lanes), x[half:].reshape(half * rows, lanes)], axis=1
    )


def unpaired(y, rows):
    lanes = y.shape[1] // 2
    return jnp.concatenate(
        [y[:, :lanes].reshape(-1, rows, lanes), y[:, lanes:].reshape(-1, rows, lanes)], axis=0
    )


def twice(square):
    zero = jnp.zeros_like(square)
    return jnp.concatenate(
        [jnp.concatenate([square, zero], axis=1), jnp.concatenate([zero, square], axis=1)], axis=0
    )


def totals_kernel(chunk, density_ref, totals_ref, brick_ref, sem):
    cells, planes, lanes = brick_ref.shape
    copies = []
    for k in range(cells // chunk):
        at = pl.ds(k * chunk, chunk)
        copies.append(pltpu.make_async_copy(density_ref.at[at], brick_ref.at[at], sem.at[k]))
        copies[-1].start()
    ones = twice(jnp.ones((lanes, lanes), jnp.bfloat16))
    lane = lax.broadcasted_iota(jnp.int32, (planes, cells), 1)
    total = jnp.zeros((planes, cells), jnp.float32)
    for k in range(cells // chunk):
        copies[k].wait()

        def step(s, total, k=k):
            first = k * chunk + s * STEP
            sums = unpaired(
                jnp.dot(
                    paired(brick_ref[pl.ds(first, STEP)], planes),
                    ones,
                    preferred_element_type=jnp.float32,
                ),
                planes,
            )
            for j in range(STEP):
                total = jnp.where(lane == first + j, sums[j], total)
            return total

        total = lax.fori_loop(0, chunk // STEP, step, total)
    totals_ref[...] = total


def local_kernel(rows, light_scale, view_scale, brick_ref, shade_ref, still_ref):
    cells, planes, lanes = brick_ref.shape
    before = lax.broadcasted_iota(jnp.int32, (lanes, lanes), 0)
    after = lax.broadcasted_iota(jnp.int32, (lanes, lanes), 1)
    earlier = twice((before < after).astype(jnp.bfloat16))
    for z in range(0, planes, rows):
        at = pl.ds(z, rows)

        def step(s, state, at=at):
            through, m1, m2, m3 = state
            first = s * STEP
            packed = brick_ref[pl.ds(first, STEP), at]
            run = unpaired(
                jnp.dot(paired(packed, rows), earlier, preferred_element_type=jnp.float32), rows
            )
            for j in range(STEP):
                value = packed[j].astype(jnp.float32)
                after = through * jnp.exp2(value * view_scale)
                weight = through - after
                through = after
                shade_ref[first + j, at] = weight * jnp.exp2(run[j] * light_scale)
                weight = weight * value
                m1 = m1 + weight
                weight = weight * value
                m2 = m2 + weight
                weight = weight * value
                m3 = m3 + weight
            return through, m1, m2, m3

        zero = jnp.zeros((rows, lanes), jnp.float32)
        through, m1, m2, m3 = lax.fori_loop(
            0, cells // STEP, step, (jnp.ones((rows, lanes), jnp.float32), zero, zero, zero)
        )
        still_ref[0, at] = through
        still_ref[1, at] = m1
        still_ref[2, at] = m2
        still_ref[3, at] = m3


def lit_kernel(rows, light_scale, coef_ref, brick_ref, shade_ref, still_ref, upstream_ref, out_ref):
    cells, planes, lanes = brick_ref.shape
    for z in range(0, planes, rows):
        at = pl.ds(z, rows)
        reach = jnp.exp2(upstream_ref[at] * light_scale)

        def step(s, state, at=at):
            reach, m0, m1, m2, m3 = state
            first = s * STEP
            packed = brick_ref[pl.ds(first, STEP), at]
            for j in range(STEP):
                value = packed[j].astype(jnp.float32)
                weight = shade_ref[first + j, at] * reach[:, j : j + 1]
                m0 = m0 + weight
                weight = weight * value
                m1 = m1 + weight
                weight = weight * value
                m2 = m2 + weight
                weight = weight * value
                m3 = m3 + weight
            return pltpu.roll(reach, cells - STEP, 1), m0, m1, m2, m3

        zero = jnp.zeros((rows, lanes), jnp.float32)
        _, m0, m1, m2, m3 = lax.fori_loop(0, cells // STEP, step, (reach, zero, zero, zero, zero))
        through = still_ref[0, at]
        m0 = m0 + 0.3 * (1.0 - through)
        m1 = m1 + 0.3 * still_ref[1, at]
        m2 = m2 + 0.3 * still_ref[2, at]
        m3 = m3 + 0.3 * still_ref[3, at]
        for c in range(3):
            out_ref[c, at] = (
                coef_ref[c, 0] * m0 + coef_ref[c, 1] * m1 + coef_ref[c, 2] * m2 + coef_ref[c, 3] * m3
            )
        out_ref[3, at] = through


def over(pieces, order):
    total = 0.0
    for a, piece in enumerate(pieces):
        ahead = jnp.ones_like(piece[3])
        for b, other in enumerate(pieces):
            if a != b:
                ahead = ahead * jnp.where(order[b] < order[a], other[3], 1.0)
        total = total + piece[:3] * ahead[None]
    return total


def body(density, color_coef):
    cells, planes, lanes = density.shape
    light_count = lax.axis_size("light")
    view_count = lax.axis_size("view")
    light_scale = -2.0 / (lanes * light_count) * LOG2E
    view_scale = -2.0 / (cells * view_count) * LOG2E
    own_rows = planes // view_count
    chunk = 16
    rows = 32
    whole = pl.BlockSpec(memory_space=VMEM)

    totals, brick = pl.pallas_call(
        functools.partial(totals_kernel, chunk),
        out_shape=[
            jax.ShapeDtypeStruct((planes, cells), jnp.float32),
            jax.ShapeDtypeStruct(density.shape, density.dtype),
        ],
        in_specs=[pl.BlockSpec(memory_space=pl.ANY)],
        out_specs=[whole, whole],
        scratch_shapes=[pltpu.SemaphoreType.DMA((cells // chunk,))],
        compiler_params=pltpu.CompilerParams(vmem_limit_bytes=8 * 2**20),
    )(density)

    place = lax.axis_index("light")
    upstream = jnp.zeros_like(totals)
    arrived = [(mask, swapped(totals, "light", mask)) for mask in range(1, light_count)]

    shade, still = pl.pallas_call(
        functools.partial(local_kernel, rows, light_scale, view_scale),
        out_shape=[
            jax.ShapeDtypeStruct(density.shape, jnp.float32),
            jax.ShapeDtypeStruct((4, planes, lanes), jnp.float32),
        ],
        in_specs=[whole],
        out_specs=[whole, whole],
        compiler_params=pltpu.CompilerParams(vmem_limit_bytes=16 * 2**20),
        cost_estimate=pl.CostEstimate(
            flops=20 * cells * planes * lanes, bytes_accessed=2**23, transcendentals=2 * cells * planes * lanes
        ),
    )(brick)

    for mask, sums in arrived:
        upstream = upstream + jnp.where(place ^ mask < place, sums, 0.0)

    partial = pl.pallas_call(
        functools.partial(lit_kernel, rows, light_scale),
        out_shape=jax.ShapeDtypeStruct((4, planes, lanes), jnp.float32),
        in_specs=[pl.BlockSpec(memory_space=pltpu.SMEM), whole, whole, whole, whole],
        out_specs=whole,
        compiler_params=pltpu.CompilerParams(vmem_limit_bytes=16 * 2**20),
    )(color_coef, brick, shade, still, upstream)

    mine = lax.axis_index("view")
    split = partial.reshape(4, view_count // 2, 2, own_rows, lanes)
    core, chip = mine % 2, mine // 2
    keep = lax.dynamic_index_in_dim(split, core, 2, False)
    give = lax.dynamic_index_in_dim(split, 1 - core, 2, False)
    took = swapped(give, "view", 1)
    near = jnp.where(core == 0, keep, took)
    far = jnp.where(core == 0, took, keep)
    color = near[:3] + near[3][None] * far[:3]
    both = jnp.concatenate([color, (near[3] * far[3])[None]], axis=0)
    pieces = [lax.dynamic_index_in_dim(both, chip, 1, False)]
    order = [chip]
    for mask in range(1, view_count // 2):
        pieces.append(swapped(lax.dynamic_index_in_dim(both, chip ^ mask, 1, False), "view", 2 * mask))
        order.append(chip ^ mask)
    return over(pieces, order)


def solution(mesh):
    placed = (P("view", None, "light"), P())
    return jax.shard_map(
        body, mesh=mesh, in_specs=placed, out_specs=P(None, "view", "light"), check_vma=False
    )
```

time: 67.8 us -> 30.1 us (0.44)
  local copies, waits for them, and re-layouts: 26.8 us -> 1.61 us
  other arithmetic: 19.1 us -> 0.7 us
  Pallas kernels: 0 us -> 13.6 us
  blocking collectives: 9.05 us -> 0 us
  waiting for transfers between devices: 0.01 us -> 4.57 us
  starting transfers between devices: 12 us -> 9.38 us
    pallas_call x0 -> x3, Pallas kernels: none -> 13.6 us  [the longest x1 5.9 us: body(): pl.pallas_call(functools.partial(local_kernel, rows, light_scale, view_sc...]
    mul x2 -> x0, local copies, waits for them, and re-layouts: 10.9 us -> none  [the longest x1 5.47 us: body(): weight = alpha * (0.3 + lit) * jnp.exp(-(view_run - view_step))]
    all_to_all x1 -> x0, blocking collectives: 9.05 us -> none  [body(): lax.all_to_all(stacked, 'view', split_axis=1, concat_axis=0, tiled=True)]
    mul x2 -> x3, other arithmetic: 8.56 us -> 0.02 us  [the longest x2 0.01 us: over(): total = total + piece[:3] * ahead[None]]
    reduce_sum x2 -> x0, other arithmetic: 5.93 us -> none  [the longest x1 5.88 us: body(): partial_value = jnp.sum(palette * weight[None], axis=1)]
    another operation x1 -> x0, local copies, waits for them, and re-layouts: 5.49 us -> none  [body(): view_run = jnp.cumsum(view_step, axis=0)]
    ppermute x3 -> x7, waiting for transfers between devices: 0.01 us -> 4.57 us  [swapped(): return lax.ppermute(x, axis, [(i, i ^ mask) for i in range(devices)])]
    unnamed x7 -> x4, local copies, waits for them, and re-layouts: 5.8 us -> 1.6 us
  transfers between devices with their start and end apart: 3 -> 7, of which waited for: 0 -> 4; matrix products, arithmetic and copies ran while one was open for 30% -> 0% of each run, Pallas kernels for 0% -> 20%
where the time goes in v1:
time: 30.1 us; the launch traced here: 30 us
  Pallas kernels  13.6 us (45%)
  starting transfers between devices  9.38 us (31%)
  waiting for transfers between devices  4.57 us (15%)
  local copies, waits for them, and re-layouts  1.61 us (5%)
  other arithmetic  0.7 us (2%)
    ppermute x7, starting transfers between devices, swapped(): return lax.ppermute(x, axis, [(i, i ^ mask) for i in range(devices)])  9.38 us
    pallas_call x1, Pallas kernels, body(): pl.pallas_call(functools.partial(local_kernel, rows, light_scale, view_sc...  5.9 us
    ppermute x7, waiting for transfers between devices, swapped(): return lax.ppermute(x, axis, [(i, i ^ mask) for i in range(devices)])  4.57 us
    pallas_call x1, Pallas kernels, body(): pl.pallas_call(functools.partial(lit_kernel, rows, light_scale), out_shap...  4.35 us
    pallas_call x1, Pallas kernels, body(): pl.pallas_call(functools.partial(totals_kernel, chunk), out_shape=[jax.Sh...  3.32 us
    unnamed x4, local copies, waits for them, and re-layouts  1.6 us
    add x1, other arithmetic, over(): total = total + piece[:3] * ahead[None]  0.61 us
  transfers between devices with their start and end apart: 7, of which 4 were waited for; matrix products, arithmetic and copies ran while one was open for 0% of the time, Pallas kernels for 20%

profile of v1, /device:TPU:0, one launch (start us, length us, event | category | flops | bytes accessed | tf_op | source)
XLA Modules:
  0.0 30.0 jit_solution(4873067997550080407)
XLA Ops:
  0.0 0.0 copy-start
  0.0 1.6 %copy-done = bf16[128,64,128]{2,1,0:T(8,128)(2,1)S(1)} copy-done((bf16[128,64,128]{2,1,0:T(8,128)(2,1)S(1)}, bf16[128,64,128]{2,1,0:T(8,128)(2,1)}, u32[]{:S(2)}) %copy-start) | copy-done | bytes 2097176
  1.6 3.3 %shard_map.28 = (f32[64,128]{1,0:T(8,128)S(1)}, bf16[128,64,128]{2,1,0:T(8,128)(2,1)S(1)}) custom-call(bf16[128,64,128]{2,1,0:T(8,128)(2,1)S(1)} %copy-done), custom_call_target="tpu_custom_call" | custom-call | tf_op jit(solution)/shard_map/pallas_call | solution.py:171
  4.9 0.0 copy-start.1
  4.9 5.1 %collective-permute-start.2 = (f32[64,128]{1,0:T(8,128)S(1)}, f32[64,128]{1,0:T(8,128)S(1)}, u32[]{:S(2)}, u32[]{:S(2)}) collective-permute-start(f32[64,128]{1,0:T(8,128)S(1)} %get-tuple-element.12), channel_id=1, source_target_pairs={{0,24},{8,16},{16,8},{24,0},{1,25},{9,17},{17,9},{25,1},{2,26},{10... | collective-permute-start | bytes 98312 | tf_op jit(solution)/shard_map/ppermute | solution.py:18
  10.0 0.0 collective-permute-start.1
  10.0 0.6 %collective-permute-start = (f32[64,128]{1,0:T(8,128)S(1)}, f32[64,128]{1,0:T(8,128)S(1)}, u32[]{:S(2)}, u32[]{:S(2)}) collective-permute-start(f32[64,128]{1,0:T(8,128)S(1)} %get-tuple-element.12), channel_id=1, source_target_pairs={{0,8},{8,0},{16,24},{24,16},{1,9},{9,1},{17,25},{25,17},{2,10},{10... | collective-permute-start | bytes 98312 | tf_op jit(solution)/shard_map/ppermute | solution.py:18
  10.7 5.9 %shard_map.29 = (f32[128,64,128]{2,1,0:T(8,128)S(1)}, f32[4,64,128]{2,1,0:T(8,128)S(1)}) custom-call(bf16[128,64,128]{2,1,0:T(8,128)(2,1)S(1)} %get-tuple-element.9.brick_ref), custom_call_target="tpu_custom_call" | custom-call | flops 20971520 | bytes 8388608 | tf_op jit(solution)/shard_map/pallas_call | solution.py:187
  16.6 0.0 collective-permute-done.2
  16.6 0.0 collective-permute-done.1
  16.6 0.0 collective-permute-done
  16.6 0.0 copy-done.1
  16.7 4.4 %shard_map.30 = f32[4,64,128]{2,1,0:T(8,128)S(1)} custom-call(f32[3,4]{1,0:T(4,128)S(1)} %copy-done.1, bf16[128,64,128]{2,1,0:T(8,128)(2,1)S(1)} %get-tuple-element.9.brick_ref, f32[128,64,128]{2,1,0:T(8,128)S(1)} %get-tuple-element.10.shade_ref, f32[4,64,128]{2,1,0:T(8,128)S(1)} %get-tuple-element.11.still_ref, f32[64,128]{1,0:T(8,128)S(1)} %select_add_fusion.upstream_ref), custom_call_target="tpu_custom_call" | custom-call | tf_op jit(solution)/shard_map/pallas_call | solution.py:204
  21.0 0.1 collective-permute-start.3
  21.2 1.2 %collective-permute-done.3 = f32[4,4,8,128]{3,2,1,0:T(8,128)S(1)} collective-permute-done((f32[4,4,8,128]{3,2,1,0:T(8,128)S(1)}, f32[4,4,8,128]{3,2,1,0:T(8,128)S(1)}, u32[]{:S(2)}, u32[]{:S(2)}) %collective-permute-start.3) | collective-permute-done | bytes 65568 | tf_op jit(solution)/shard_map/ppermute | solution.py:18
  22.4 2.7 %collective-permute-start.6 = (f32[4,8,128]{2,1,0:T(8,128)S(1)}, f32[4,8,128]{2,1,0:T(8,128)S(1)}, u32[]{:S(2)}, u32[]{:S(2)}) collective-permute-start(f32[4,8,128]{2,1,0:T(8,128)S(1)} %get-tuple-element.18), channel_id=1, source_target_pairs={{0,6},{1,7},{2,4},{3,5},{4,2},{5,3},{6,0},{7,1},{8,14},{9,15},{10,... | collective-permute-start | bytes 49160 | tf_op jit(solution)/shard_map/ppermute | solution.py:18
  25.1 0.5 %collective-permute-start.4 = (f32[4,8,128]{2,1,0:T(8,128)S(1)}, f32[4,8,128]{2,1,0:T(8,128)S(1)}, u32[]{:S(2)}, u32[]{:S(2)}) collective-permute-start(f32[4,8,128]{2,1,0:T(8,128)S(1)} %get-tuple-element.16), channel_id=1, source_target_pairs={{0,2},{1,3},{2,0},{3,1},{4,6},{5,7},{6,4},{7,5},{8,10},{9,11},{10,... | collective-permute-start | bytes 49160 | tf_op jit(solution)/shard_map/ppermute | solution.py:18
  25.6 0.4 %collective-permute-start.5 = (f32[4,8,128]{2,1,0:T(8,128)S(1)}, f32[4,8,128]{2,1,0:T(8,128)S(1)}, u32[]{:S(2)}, u32[]{:S(2)}) collective-permute-start(f32[4,8,128]{2,1,0:T(8,128)S(1)} %get-tuple-element.17), channel_id=1, source_target_pairs={{0,4},{1,5},{2,6},{3,7},{4,0},{5,1},{6,2},{7,3},{8,12},{9,13},{10,... | collective-permute-start | bytes 49160 | tf_op jit(solution)/shard_map/ppermute | solution.py:18
  26.0 1.1 %collective-permute-done.6 = f32[4,8,128]{2,1,0:T(8,128)S(1)} collective-permute-done((f32[4,8,128]{2,1,0:T(8,128)S(1)}, f32[4,8,128]{2,1,0:T(8,128)S(1)}, u32[]{:S(2)}, u32[]{:S(2)}) %collective-permute-start.6) | collective-permute-done | bytes 16416 | tf_op jit(solution)/shard_map/ppermute | solution.py:18
  27.1 1.7 %collective-permute-done.4 = f32[4,8,128]{2,1,0:T(8,128)S(1)} collective-permute-done((f32[4,8,128]{2,1,0:T(8,128)S(1)}, f32[4,8,128]{2,1,0:T(8,128)S(1)}, u32[]{:S(2)}, u32[]{:S(2)}) %collective-permute-start.4) | collective-permute-done | bytes 16416 | tf_op jit(solution)/shard_map/ppermute | solution.py:18
  28.8 0.5 %collective-permute-done.5 = f32[4,8,128]{2,1,0:T(8,128)S(1)} collective-permute-done((f32[4,8,128]{2,1,0:T(8,128)S(1)}, f32[4,8,128]{2,1,0:T(8,128)S(1)}, u32[]{:S(2)}, u32[]{:S(2)}) %collective-permute-start.5) | collective-permute-done | bytes 16416 | tf_op jit(solution)/shard_map/ppermute | solution.py:18
  29.4 0.6 %fusion.8 = f32[3,8,128]{2,1,0:T(8,128)} fusion(f32[4,8,128]{2,1,0:T(8,128)S(1)} %collective-permute-done.6, f32[4,8,128]{2,1,0:T(8,128)S(1)} %collective-permute-done.5, f32[4,8,128]{2,1,0:T(8,128)S(1)} %collective-permute-done.4, f32[4,1,8,128]{3,2,1,0:T(8,128)S(1)} %get-tuple-element.15, f32[8,128]{1,0:T(8,128)S(1)} %get-tuple-element.22, ...), kind=kLoop, calls=%fused_computation.24 | loop fusion | flops 21504 | bytes 77824 | tf_op jit(solution)/shard_map/add | solution.py:156
  (8 shorter events, 0.1 us)
Async XLA Ops:
  0.0 1.6 %copy-start = (bf16[128,64,128]{2,1,0:T(8,128)(2,1)S(1)}, bf16[128,64,128]{2,1,0:T(8,128)(2,1)}, u32[]{:S(2)}) copy-start(bf16[128,64,128]{2,1,0:T(8,128)(2,1)} %density_ref.1) | copy-start | bytes 6291460
  4.9 11.7 %copy-start.1 = (f32[3,4]{1,0:T(4,128)S(1)}, f32[3,4]{1,0:T(4,128)}, u32[]{:S(2)}) copy-start(f32[3,4]{1,0:T(4,128)} %coef_ref.1) | copy-start | bytes 148
  4.9 11.7 %collective-permute-start.2 = (f32[64,128]{1,0:T(8,128)S(1)}, f32[64,128]{1,0:T(8,128)S(1)}, u32[]{:S(2)}, u32[]{:S(2)}) collective-permute-start(f32[64,128]{1,0:T(8,128)S(1)} %get-tuple-element.12), channel_id=1, source_target_pairs={{0,24},{8,16},{16,8},{24,0},{1,25},{9,17},{17,9},{25,1},{2,26},{10... | collective-permute-start | bytes 98312 | tf_op jit(solution)/shard_map/ppermute | solution.py:18
  10.0 6.6 %collective-permute-start.1 = (f32[64,128]{1,0:T(8,128)S(1)}, f32[64,128]{1,0:T(8,128)S(1)}, u32[]{:S(2)}, u32[]{:S(2)}) collective-permute-start(f32[64,128]{1,0:T(8,128)S(1)} %get-tuple-element.12), channel_id=1, source_target_pairs={{0,16},{8,24},{16,0},{24,8},{1,17},{9,25},{17,1},{25,9},{2,18},{10... | collective-permute-start | bytes 98312 | tf_op jit(solution)/shard_map/ppermute | solution.py:18
  10.0 6.6 %collective-permute-start = (f32[64,128]{1,0:T(8,128)S(1)}, f32[64,128]{1,0:T(8,128)S(1)}, u32[]{:S(2)}, u32[]{:S(2)}) collective-permute-start(f32[64,128]{1,0:T(8,128)S(1)} %get-tuple-element.12), channel_id=1, source_target_pairs={{0,8},{8,0},{16,24},{24,16},{1,9},{9,1},{17,25},{25,17},{2,10},{10... | collective-permute-start | bytes 98312 | tf_op jit(solution)/shard_map/ppermute | solution.py:18
  21.0 1.3 %collective-permute-start.3 = (f32[4,4,8,128]{3,2,1,0:T(8,128)S(1)}, f32[4,4,8,128]{3,2,1,0:T(8,128)S(1)}, u32[]{:S(2)}, u32[]{:S(2)}) collective-permute-start(f32[4,4,8,128]{3,2,1,0:T(8,128)S(1)} %dynamic-slice_bitcast_fusion), channel_id=1, source_target_pairs={{0,1},{1,0},{2,3},{3,2},{4,5},{5,4},{6,7},{7,6},{8,9},{9,8},{10,11... | collective-permute-start | bytes 196616 | tf_op jit(solution)/shard_map/ppermute | solution.py:18
  22.4 4.7 %collective-permute-start.6 = (f32[4,8,128]{2,1,0:T(8,128)S(1)}, f32[4,8,128]{2,1,0:T(8,128)S(1)}, u32[]{:S(2)}, u32[]{:S(2)}) collective-permute-start(f32[4,8,128]{2,1,0:T(8,128)S(1)} %get-tuple-element.18), channel_id=1, source_target_pairs={{0,6},{1,7},{2,4},{3,5},{4,2},{5,3},{6,0},{7,1},{8,14},{9,15},{10,... | collective-permute-start | bytes 49160 | tf_op jit(solution)/shard_map/ppermute | solution.py:18
  25.1 3.7 %collective-permute-start.4 = (f32[4,8,128]{2,1,0:T(8,128)S(1)}, f32[4,8,128]{2,1,0:T(8,128)S(1)}, u32[]{:S(2)}, u32[]{:S(2)}) collective-permute-start(f32[4,8,128]{2,1,0:T(8,128)S(1)} %get-tuple-element.16), channel_id=1, source_target_pairs={{0,2},{1,3},{2,0},{3,1},{4,6},{5,7},{6,4},{7,5},{8,10},{9,11},{10,... | collective-permute-start | bytes 49160 | tf_op jit(solution)/shard_map/ppermute | solution.py:18
  25.6 3.7 %collective-permute-start.5 = (f32[4,8,128]{2,1,0:T(8,128)S(1)}, f32[4,8,128]{2,1,0:T(8,128)S(1)}, u32[]{:S(2)}, u32[]{:S(2)}) collective-permute-start(f32[4,8,128]{2,1,0:T(8,128)S(1)} %get-tuple-element.17), channel_id=1, source_target_pairs={{0,4},{1,5},{2,6},{3,7},{4,0},{5,1},{6,2},{7,3},{8,12},{9,13},{10,... | collective-permute-start | bytes 49160 | tf_op jit(solution)/shard_map/ppermute | solution.py:18

commit v2 on v0

v2 whole, which is shorter than its diff:
```python
import functools
import math

import jax
import jax.numpy as jnp
import ml_dtypes
from jax import lax
from jax.experimental import pallas as pl
from jax.experimental.pallas import tpu as pltpu
from jax.sharding import PartitionSpec as P

VMEM = pltpu.VMEM
LOG2E = math.log2(math.e)
HEIGHT = 16


def swapped(x, axis, mask):
    devices = lax.axis_size(axis)
    return lax.ppermute(x, axis, [(i, i ^ mask) for i in range(devices)])


def in_parts(scale):
    high = float(ml_dtypes.bfloat16(scale))
    return high, float(ml_dtypes.bfloat16(scale - high))


def stacked(pattern, parts):
    return jnp.concatenate(
        [jnp.where(pattern, part, 0.0).astype(jnp.bfloat16) for part in parts], axis=0
    )


def totals_kernel(chunk, density_ref, totals_ref, brick_ref, sem):
    cells, planes, lanes = brick_ref.shape
    half = cells // 2
    copies = []
    for k in range(half // chunk):
        for first in (k * chunk, half + k * chunk):
            at = pl.ds(first, chunk)
            copies.append(
                pltpu.make_async_copy(density_ref.at[at], brick_ref.at[at], sem.at[len(copies)])
            )
            copies[-1].start()
    row = lax.broadcasted_iota(jnp.int32, (16, 2 * lanes), 0)
    column = lax.broadcasted_iota(jnp.int32, (16, 2 * lanes), 1)
    pick = jnp.where(row == column // lanes, 1.0, 0.0).astype(jnp.bfloat16)

    def pair(v):
        return [brick_ref[v], brick_ref[half + v]]

    for k in range(half // chunk):
        copies[2 * k].wait()
        copies[2 * k + 1].wait()
        for v in range(k * chunk, (k + 1) * chunk, 4):
            left = jnp.concatenate(pair(v) + pair(v + 1), axis=0)
            right = jnp.concatenate(pair(v + 2) + pair(v + 3), axis=0)
            sums = lax.dot_general(
                pick,
                jnp.concatenate([left, right], axis=1),
                (((1,), (1,)), ((), ())),
                preferred_element_type=jnp.float32,
            )
            for j in range(4):
                at = pl.ds(j % 2 * 2 * planes, 2 * planes)
                totals_ref[v + j : v + j + 1] = sums[j // 2 : j // 2 + 1, at.start : at.start + at.size]


def local_kernel(rows, step_cells, light_parts, view_parts, brick_ref, *refs):
    shade_ref, value_ref, still_ref, even, odd = refs
    cells, planes, lanes = brick_ref.shape
    chunks = cells // step_cells
    before = lax.broadcasted_iota(jnp.int32, (lanes, lanes), 0)
    after = lax.broadcasted_iota(jnp.int32, (lanes, lanes), 1)
    depths = jnp.concatenate(
        [stacked(before < after, light_parts), stacked(before == after, view_parts)], axis=1
    )

    def fill(chunk, at, buffer):
        packed = brick_ref[pl.ds(chunk * step_cells, step_cells), at]
        flat = packed.reshape(step_cells * rows, lanes)
        depth = jnp.dot(
            jnp.concatenate([flat, flat], axis=1), depths, preferred_element_type=jnp.float32
        )
        buffer[0] = jnp.exp2(depth[:, :lanes])
        buffer[1] = jnp.exp2(depth[:, lanes:])
        buffer[2] = depth[:, lanes:]

    def use(chunk, at, buffer, state):
        through, m1, m2, m3 = state
        for j in range(step_cells):
            cell = chunk * step_cells + j
            here = pl.ds(j * rows, rows)
            value = buffer[2, here]
            passed = through * buffer[1, here]
            weight = through - passed
            through = passed
            value_ref[cell, at] = value
            shade_ref[cell, at] = weight * buffer[0, here]
            weight = weight * value
            m1 = m1 + weight
            weight = weight * value
            m2 = m2 + weight
            weight = weight * value
            m3 = m3 + weight
        return through, m1, m2, m3

    blocks = [pl.ds(z, rows) for z in range(0, planes, rows)]
    fill(0, blocks[0], even)
    for k, at in enumerate(blocks):
        zero = jnp.zeros((rows, lanes), jnp.float32)
        state = (jnp.ones((rows, lanes), jnp.float32), zero, zero, zero)
        for chunk in range(0, chunks, 2):
            fill(chunk + 1, at, odd)
            state = use(chunk, at, even, state)
            if chunk + 2 < chunks:
                fill(chunk + 2, at, even)
            elif k + 1 < len(blocks):
                fill(0, blocks[k + 1], even)
            state = use(chunk + 1, at, odd, state)
        for i in range(4):
            still_ref[i, at] = state[i]


def lit_kernel(
    step_cells,
    light_scale,
    unit,
    coef_ref,
    light_ref,
    still_ref,
    shade_ref,
    value_ref,
    out_ref,
    reach_ref,
    even,
    odd,
):
    cells, planes, lanes = shade_ref.shape
    blocks = planes // HEIGHT
    chunks = cells // step_cells
    reach = jnp.exp2(light_ref[...] * light_scale).T
    half = reach.shape[0] // 2
    reach_ref[...] = jnp.concatenate([reach[:half], reach[half:]], axis=1)
    pair = lax.broadcasted_iota(jnp.int32, (HEIGHT, cells), 1) // 2
    row = lax.broadcasted_iota(jnp.int32, (2 * cells, 2 * lanes), 0)
    column = lax.broadcasted_iota(jnp.int32, (2 * cells, 2 * lanes), 1)
    turns = jnp.where((row % 2 == 0) == (column < lanes), 1.0, 0.0).astype(jnp.bfloat16)

    def parts(k):
        reach = reach_ref[pl.ds(k * HEIGHT, HEIGHT)]
        high = reach.astype(jnp.bfloat16)
        return high, (reach - high.astype(jnp.float32)).astype(jnp.bfloat16)

    def fill(chunk, both, buffer):
        first = chunk * step_cells // 2
        picked = [
            jnp.concatenate([jnp.where(pair == first + p, part, 0) for part in both], axis=1)
            for p in range(step_cells // 2)
        ]
        spread = jnp.dot(
            jnp.concatenate(picked, axis=0), turns, preferred_element_type=jnp.float32
        )
        buffer[0] = spread[:, :lanes]
        buffer[1] = spread[:, lanes:]

    def use(chunk, k, buffer, state):
        m0, m1, m2, m3 = state
        at = pl.ds(k * HEIGHT, HEIGHT)
        for j in range(step_cells):
            cell = chunk * step_cells + j
            value = value_ref[cell, at]
            weight = shade_ref[cell, at] * buffer[j % 2, pl.ds(j // 2 * HEIGHT, HEIGHT)]
            m0 = m0 + weight
            weight = weight * value
            m1 = m1 + weight
            weight = weight * value
            m2 = m2 + weight
            weight = weight * value
            m3 = m3 + weight
        return m0, m1, m2, m3

    both = parts(0)
    fill(0, both, even)
    for k in range(blocks):
        state = (jnp.zeros((HEIGHT, lanes), jnp.float32),) * 4
        for chunk in range(0, chunks, 2):
            fill(chunk + 1, both, odd)
            state = use(chunk, k, even, state)
            if chunk + 2 < chunks:
                fill(chunk + 2, both, even)
            elif k + 1 < blocks:
                both = parts(k + 1)
                fill(0, both, even)
            state = use(chunk + 1, k, odd, state)
        at = pl.ds(k * HEIGHT, HEIGHT)
        through = still_ref[0, at]
        m0 = state[0] + 0.3 * (1.0 - through)
        m1, m2, m3 = (state[i] + 0.3 * still_ref[i, at] for i in (1, 2, 3))
        for c in range(3):
            out_ref[k, c] = (
                coef_ref[c, 0] * m0
                + coef_ref[c, 1] * unit * m1
                + coef_ref[c, 2] * unit**2 * m2
                + coef_ref[c, 3] * unit**3 * m3
            )
        out_ref[k, 3] = through


def over(pieces, order):
    total = 0.0
    for a, piece in enumerate(pieces):
        ahead = jnp.ones_like(piece[3])
        for b, other in enumerate(pieces):
            if a != b:
                ahead = ahead * jnp.where(order[b] < order[a], other[3], 1.0)
        total = total + piece[:3] * ahead[None]
    return total


def body(density, color_coef):
    cells, planes, lanes = density.shape
    light_count = lax.axis_size("light")
    view_count = lax.axis_size("view")
    light_scale = -2.0 / (lanes * light_count) * LOG2E
    view_parts = in_parts(-2.0 / (cells * view_count) * LOG2E)
    own_rows = planes // view_count
    chunk = 32
    step_cells = 16
    rows = 32
    lit_cells = 16
    whole = pl.BlockSpec(memory_space=VMEM)
    scalars = pl.BlockSpec(memory_space=pltpu.SMEM)

    totals, brick = pl.pallas_call(
        functools.partial(totals_kernel, chunk),
        name="totals_kernel",
        out_shape=[
            jax.ShapeDtypeStruct((cells // 2, 2 * planes), jnp.float32),
            jax.ShapeDtypeStruct(density.shape, density.dtype),
        ],
        in_specs=[pl.BlockSpec(memory_space=pltpu.HBM)],
        out_specs=[whole, whole],
        scratch_shapes=[pltpu.SemaphoreType.DMA((cells // chunk,))],
        compiler_params=pltpu.CompilerParams(vmem_limit_bytes=50 * 2**20 + 2**19),
    )(density)

    place = lax.axis_index("light")
    arrived = [(mask, swapped(totals, "light", mask)) for mask in range(1, light_count)]

    mine = lax.axis_index("view")
    core, chip = mine % 2, mine // 2
    chips = view_count // 2
    others = list(range(1, chips))
    table = jax.ShapeDtypeStruct(density.shape, jnp.float32)
    shade, value, still = pl.pallas_call(
        functools.partial(local_kernel, rows, step_cells, in_parts(light_scale), view_parts),
        name="local_kernel",
        out_shape=[table, table, jax.ShapeDtypeStruct((4, planes, lanes), jnp.float32)],
        in_specs=[whole],
        out_specs=[whole] * 3,
        scratch_shapes=[VMEM((3, step_cells * rows, lanes), jnp.float32)] * 2,
        compiler_params=pltpu.CompilerParams(vmem_limit_bytes=8 * 2**20),
        cost_estimate=pl.CostEstimate(
            flops=20 * density.size, bytes_accessed=2**23, transcendentals=2 * density.size
        ),
    )(brick)

    upstream = jnp.zeros_like(totals)
    for mask, other in arrived:
        upstream = upstream + jnp.where(place ^ mask < place, other, 0.0)

    away = pl.pallas_call(
        functools.partial(lit_kernel, lit_cells, light_scale, 1.0 / sum(view_parts)),
        name="lit_kernel",
        out_shape=jax.ShapeDtypeStruct((planes // HEIGHT, 4, HEIGHT, lanes), jnp.float32),
        in_specs=[scalars] + [whole] * 4,
        out_specs=whole,
        scratch_shapes=[VMEM((planes, cells), jnp.float32)]
        + [VMEM((2, lit_cells // 2 * HEIGHT, lanes), jnp.float32)] * 2,
        compiler_params=pltpu.CompilerParams(vmem_limit_bytes=8 * 2**20),
    )(color_coef, upstream, still, shade, value)

    if 2 * own_rows != HEIGHT:
        away = jnp.swapaxes(away, 0, 1).reshape(4, chips, 2 * own_rows, lanes)
        away = jnp.swapaxes(away, 0, 1)
    sent = [lax.dynamic_index_in_dim(away, chip ^ mask, 0, False) for mask in others]
    own = lax.dynamic_index_in_dim(away, chip, 0, False)
    pieces = [own] + [swapped(x, "view", 2 * mask) for x, mask in zip(sent, others)]
    order = [chip] + [chip ^ mask for mask in others]
    pieces = jnp.stack(pieces).reshape(chips, 4, 2, own_rows, lanes)
    keep = lax.dynamic_index_in_dim(pieces, core, 2, False)
    took = swapped(lax.dynamic_index_in_dim(pieces, 1 - core, 2, False), "view", 1)
    near = jnp.where(core == 0, keep, took)
    far = jnp.where(core == 0, took, keep)
    color = near[:, :3] + near[:, 3:] * far[:, :3]
    both = jnp.concatenate([color, near[:, 3:] * far[:, 3:]], axis=1)
    return over([both[k] for k in range(chips)], order)


def solution(mesh):
    placed = (P("view", None, "light"), P())
    return jax.shard_map(
        body, mesh=mesh, in_specs=placed, out_specs=P(None, "view", "light"), check_vma=False
    )
```

time: 67.8 us -> 23.5 us (0.35)
  local copies, waits for them, and re-layouts: 26.8 us -> 0.04 us
  other arithmetic: 19.1 us -> 0.68 us
  blocking collectives: 9.05 us -> 0 us
  waiting for transfers between devices: 0.01 us -> 6.59 us
  Pallas kernels: 0 us -> 6.52 us
  starting transfers between devices: 12 us -> 9.38 us
    mul x2 -> x0, local copies, waits for them, and re-layouts: 10.9 us -> none  [the longest x1 5.47 us: body(): weight = alpha * (0.3 + lit) * jnp.exp(-(view_run - view_step))]
    all_to_all x1 -> x0, blocking collectives: 9.05 us -> none  [body(): lax.all_to_all(stacked, 'view', split_axis=1, concat_axis=0, tiled=True)]
    mul x2 -> x3, other arithmetic: 8.56 us -> 0.03 us  [the longest x2 0.02 us: over(): ahead = ahead * jnp.where(order[b] < order[a], other[3], 1.0)]
    ppermute x3 -> x7, waiting for transfers between devices: 0.01 us -> 6.59 us  [swapped(): return lax.ppermute(x, axis, [(i, i ^ mask) for i in range(devices)])]
    pallas_call x0 -> x3, Pallas kernels: none -> 6.52 us  [the longest x1 2.36 us: body(): pl.pallas_call(functools.partial(lit_kernel, lit_cells, light_scale, 1.0...]
    reduce_sum x2 -> x0, other arithmetic: 5.93 us -> none  [the longest x1 5.88 us: body(): partial_value = jnp.sum(palette * weight[None], axis=1)]
    unnamed x7 -> x2, local copies, waits for them, and re-layouts: 5.8 us -> 0.01 us
    another operation x1, local copies, waits for them, and re-layouts: 5.49 us -> 0.02 us  [body(): pieces = jnp.stack(pieces).reshape(chips, 4, 2, own_rows, lanes)]
  transfers between devices with their start and end apart: 3 -> 7, of which waited for: 0 -> 5; matrix products, arithmetic and copies ran while one was open for 30% -> 0% of each run, Pallas kernels for 0% -> 9%
where the time goes in v2:
time: 23.5 us; the launch traced here: 23.4 us
  starting transfers between devices  9.38 us (40%)
  waiting for transfers between devices  6.59 us (28%)
  Pallas kernels  6.52 us (28%)
  other arithmetic  0.68 us (3%)
    ppermute x7, starting transfers between devices, swapped(): return lax.ppermute(x, axis, [(i, i ^ mask) for i in range(devices)])  9.38 us
    ppermute x7, waiting for transfers between devices, swapped(): return lax.ppermute(x, axis, [(i, i ^ mask) for i in range(devices)])  6.59 us
    pallas_call x1, Pallas kernels, body(): pl.pallas_call(functools.partial(lit_kernel, lit_cells, light_scale, 1.0...  2.36 us
    pallas_call x1, Pallas kernels, body(): pl.pallas_call(functools.partial(local_kernel, rows, step_cells, in_parts...  2.14 us
    pallas_call x1, Pallas kernels, body(): pl.pallas_call(functools.partial(totals_kernel, chunk), name='totals_kern...  2.02 us
    add x1, other arithmetic, over(): total = total + piece[:3] * ahead[None]  0.61 us
  transfers between devices with their start and end apart: 7, of which 5 were waited for; matrix products, arithmetic and copies ran while one was open for 0% of the time, Pallas kernels for 9%

profile of v2, /device:TPU:0, one launch (start us, length us, event | category | flops | bytes accessed | tf_op | source)
XLA Modules:
  0.0 23.4 jit_solution(6343262669471012928)
XLA Ops:
  0.0 0.0 copy-start
  0.0 2.0 %totals_kernel.1 = (f32[64,128]{1,0:T(8,128)S(1)}, bf16[128,64,128]{2,1,0:T(8,128)(2,1)S(1)}) custom-call(bf16[128,64,128]{2,1,0:T(8,128)(2,1)} %density_ref.1), custom_call_target="tpu_custom_call" | custom-call | tf_op jit(solution)/shard_map/totals_kernel/pallas_call | solution.py:234
  2.0 5.1 %collective-permute-start.2 = (f32[64,128]{1,0:T(8,128)S(1)}, f32[64,128]{1,0:T(8,128)S(1)}, u32[]{:S(2)}, u32[]{:S(2)}) collective-permute-start(f32[64,128]{1,0:T(8,128)S(1)} %get-tuple-element.10), channel_id=1, source_target_pairs={{0,24},{8,16},{16,8},{24,0},{1,25},{9,17},{17,9},{25,1},{2,26},{10... | collective-permute-start | bytes 98312 | tf_op jit(solution)/shard_map/ppermute | solution.py:19
  7.2 0.0 collective-permute-start.1
  7.2 0.6 %collective-permute-start = (f32[64,128]{1,0:T(8,128)S(1)}, f32[64,128]{1,0:T(8,128)S(1)}, u32[]{:S(2)}, u32[]{:S(2)}) collective-permute-start(f32[64,128]{1,0:T(8,128)S(1)} %get-tuple-element.10), channel_id=1, source_target_pairs={{0,8},{8,0},{16,24},{24,16},{1,9},{9,1},{17,25},{25,17},{2,10},{10... | collective-permute-start | bytes 98312 | tf_op jit(solution)/shard_map/ppermute | solution.py:19
  7.8 2.1 %local_kernel.1 = (f32[128,64,128]{2,1,0:T(8,128)S(1)}, f32[128,64,128]{2,1,0:T(8,128)S(1)}, f32[4,64,128]{2,1,0:T(8,128)S(1)}) custom-call(bf16[128,64,128]{2,1,0:T(8,128)(2,1)S(1)} %get-tuple-element.11.brick_ref), custom_call_target="tpu_custom_call" | custom-call | flops 20971520 | bytes 8388608 | tf_op jit(solution)/shard_map/local_kernel/pallas_call | solution.py:255
  9.9 0.0 collective-permute-done.2
  10.0 2.0 %collective-permute-done.1 = f32[64,128]{1,0:T(8,128)S(1)} collective-permute-done((f32[64,128]{1,0:T(8,128)S(1)}, f32[64,128]{1,0:T(8,128)S(1)}, u32[]{:S(2)}, u32[]{:S(2)}) %collective-permute-start.1) | collective-permute-done | bytes 32800 | tf_op jit(solution)/shard_map/ppermute | solution.py:19
  12.0 0.0 collective-permute-done
  12.0 0.0 copy-done
  12.0 2.4 %lit_kernel.1 = f32[4,4,16,128]{3,2,1,0:T(8,128)S(1)} custom-call(f32[3,4]{1,0:T(4,128)S(1)} %copy-done, f32[64,128]{1,0:T(8,128)S(1)} %select_add_fusion.light_ref, f32[4,64,128]{2,1,0:T(8,128)S(1)} %get-tuple-element.12.still_ref, f32[128,64,128]{2,1,0:T(8,128)S(1)} %get-tuple-element.13.shade_ref, f32[128,64,128]{2,1,0:T(8,128)S(1)} %get-tuple-element.14.value_ref), custom_call_target="tpu_custom_call" | custom-call | tf_op jit(solution)/shard_map/lit_kernel/pallas_call | solution.py:272
  14.4 2.5 %collective-permute-start.5 = (f32[4,16,128]{2,1,0:T(8,128)S(1)}, f32[4,16,128]{2,1,0:T(8,128)S(1)}, u32[]{:S(2)}, u32[]{:S(2)}) collective-permute-start(f32[4,16,128]{2,1,0:T(8,128)S(1)} %get-tuple-element.18), channel_id=1, source_target_pairs={{0,6},{1,7},{2,4},{3,5},{4,2},{5,3},{6,0},{7,1},{8,14},{9,15},{10,... | collective-permute-start | bytes 98312 | tf_op jit(solution)/shard_map/ppermute | solution.py:19
  16.9 0.5 %collective-permute-start.4 = (f32[4,16,128]{2,1,0:T(8,128)S(1)}, f32[4,16,128]{2,1,0:T(8,128)S(1)}, u32[]{:S(2)}, u32[]{:S(2)}) collective-permute-start(f32[4,16,128]{2,1,0:T(8,128)S(1)} %get-tuple-element.19), channel_id=1, source_target_pairs={{0,4},{1,5},{2,6},{3,7},{4,0},{5,1},{6,2},{7,3},{8,12},{9,13},{10,... | collective-permute-start | bytes 98312 | tf_op jit(solution)/shard_map/ppermute | solution.py:19
  17.4 0.5 %collective-permute-start.3 = (f32[4,16,128]{2,1,0:T(8,128)S(1)}, f32[4,16,128]{2,1,0:T(8,128)S(1)}, u32[]{:S(2)}, u32[]{:S(2)}) collective-permute-start(f32[4,16,128]{2,1,0:T(8,128)S(1)} %get-tuple-element.20), channel_id=1, source_target_pairs={{0,2},{1,3},{2,0},{3,1},{4,6},{5,7},{6,4},{7,5},{8,10},{9,11},{10,... | collective-permute-start | bytes 98312 | tf_op jit(solution)/shard_map/ppermute | solution.py:19
  17.9 1.6 %collective-permute-done.5 = f32[4,16,128]{2,1,0:T(8,128)S(1)} collective-permute-done((f32[4,16,128]{2,1,0:T(8,128)S(1)}, f32[4,16,128]{2,1,0:T(8,128)S(1)}, u32[]{:S(2)}, u32[]{:S(2)}) %collective-permute-start.5) | collective-permute-done | bytes 32800 | tf_op jit(solution)/shard_map/ppermute | solution.py:19
  19.5 1.3 %collective-permute-done.4 = f32[4,16,128]{2,1,0:T(8,128)S(1)} collective-permute-done((f32[4,16,128]{2,1,0:T(8,128)S(1)}, f32[4,16,128]{2,1,0:T(8,128)S(1)}, u32[]{:S(2)}, u32[]{:S(2)}) %collective-permute-start.4) | collective-permute-done | bytes 32800 | tf_op jit(solution)/shard_map/ppermute | solution.py:19
  20.8 0.5 %collective-permute-done.3 = f32[4,16,128]{2,1,0:T(8,128)S(1)} collective-permute-done((f32[4,16,128]{2,1,0:T(8,128)S(1)}, f32[4,16,128]{2,1,0:T(8,128)S(1)}, u32[]{:S(2)}, u32[]{:S(2)}) %collective-permute-start.3) | collective-permute-done | bytes 32800 | tf_op jit(solution)/shard_map/ppermute | solution.py:19
  21.4 0.1 collective-permute-start.6
  21.5 1.2 %collective-permute-done.6 = f32[4,4,8,128]{3,2,1,0:T(8,128)S(1)} collective-permute-done((f32[4,4,8,128]{3,2,1,0:T(8,128)S(1)}, f32[4,4,8,128]{3,2,1,0:T(8,128)S(1)}, u32[]{:S(2)}, u32[]{:S(2)}) %collective-permute-start.6) | collective-permute-done | bytes 65568 | tf_op jit(solution)/shard_map/ppermute | solution.py:19
  22.8 0.6 %fusion.2 = f32[3,8,128]{2,1,0:T(8,128)} fusion(f32[4,3,8,128]{3,2,1,0:T(8,128)S(1)} %fusion, f32[8,128]{1,0:T(8,128)S(1)} %multiply_bitcast_fusion, f32[8,128]{1,0:T(8,128)S(1)} %get-tuple-element.25, f32[8,128]{1,0:T(8,128)S(1)} %get-tuple-element.24, f32[8,128]{1,0:T(8,128)S(1)} %get-tuple-element.23), kind=kLoop, calls=%fused_computation.15 | loop fusion | flops 21504 | bytes 77824 | tf_op jit(solution)/shard_map/add | solution.py:216
  (9 shorter events, 0.1 us)
Async XLA Ops:
  0.0 12.0 %copy-start = (f32[3,4]{1,0:T(4,128)S(1)}, f32[3,4]{1,0:T(4,128)}, u32[]{:S(2)}) copy-start(f32[3,4]{1,0:T(4,128)} %coef_ref.1) | copy-start | bytes 148
  2.0 7.9 %collective-permute-start.2 = (f32[64,128]{1,0:T(8,128)S(1)}, f32[64,128]{1,0:T(8,128)S(1)}, u32[]{:S(2)}, u32[]{:S(2)}) collective-permute-start(f32[64,128]{1,0:T(8,128)S(1)} %get-tuple-element.10), channel_id=1, source_target_pairs={{0,24},{8,16},{16,8},{24,0},{1,25},{9,17},{17,9},{25,1},{2,26},{10... | collective-permute-start | bytes 98312 | tf_op jit(solution)/shard_map/ppermute | solution.py:19
  7.2 4.8 %collective-permute-start.1 = (f32[64,128]{1,0:T(8,128)S(1)}, f32[64,128]{1,0:T(8,128)S(1)}, u32[]{:S(2)}, u32[]{:S(2)}) collective-permute-start(f32[64,128]{1,0:T(8,128)S(1)} %get-tuple-element.10), channel_id=1, source_target_pairs={{0,16},{8,24},{16,0},{24,8},{1,17},{9,25},{17,1},{25,9},{2,18},{10... | collective-permute-start | bytes 98312 | tf_op jit(solution)/shard_map/ppermute | solution.py:19
  7.2 4.8 %collective-permute-start = (f32[64,128]{1,0:T(8,128)S(1)}, f32[64,128]{1,0:T(8,128)S(1)}, u32[]{:S(2)}, u32[]{:S(2)}) collective-permute-start(f32[64,128]{1,0:T(8,128)S(1)} %get-tuple-element.10), channel_id=1, source_target_pairs={{0,8},{8,0},{16,24},{24,16},{1,9},{9,1},{17,25},{25,17},{2,10},{10... | collective-permute-start | bytes 98312 | tf_op jit(solution)/shard_map/ppermute | solution.py:19
  14.4 5.1 %collective-permute-start.5 = (f32[4,16,128]{2,1,0:T(8,128)S(1)}, f32[4,16,128]{2,1,0:T(8,128)S(1)}, u32[]{:S(2)}, u32[]{:S(2)}) collective-permute-start(f32[4,16,128]{2,1,0:T(8,128)S(1)} %get-tuple-element.18), channel_id=1, source_target_pairs={{0,6},{1,7},{2,4},{3,5},{4,2},{5,3},{6,0},{7,1},{8,14},{9,15},{10,... | collective-permute-start | bytes 98312 | tf_op jit(solution)/shard_map/ppermute | solution.py:19
  16.9 3.9 %collective-permute-start.4 = (f32[4,16,128]{2,1,0:T(8,128)S(1)}, f32[4,16,128]{2,1,0:T(8,128)S(1)}, u32[]{:S(2)}, u32[]{:S(2)}) collective-permute-start(f32[4,16,128]{2,1,0:T(8,128)S(1)} %get-tuple-element.19), channel_id=1, source_target_pairs={{0,4},{1,5},{2,6},{3,7},{4,0},{5,1},{6,2},{7,3},{8,12},{9,13},{10,... | collective-permute-start | bytes 98312 | tf_op jit(solution)/shard_map/ppermute | solution.py:19
  17.4 3.9 %collective-permute-start.3 = (f32[4,16,128]{2,1,0:T(8,128)S(1)}, f32[4,16,128]{2,1,0:T(8,128)S(1)}, u32[]{:S(2)}, u32[]{:S(2)}) collective-permute-start(f32[4,16,128]{2,1,0:T(8,128)S(1)} %get-tuple-element.20), channel_id=1, source_target_pairs={{0,2},{1,3},{2,0},{3,1},{4,6},{5,7},{6,4},{7,5},{8,10},{9,11},{10,... | collective-permute-start | bytes 98312 | tf_op jit(solution)/shard_map/ppermute | solution.py:19
  21.4 1.3 %collective-permute-start.6 = (f32[4,4,8,128]{3,2,1,0:T(8,128)S(1)}, f32[4,4,8,128]{3,2,1,0:T(8,128)S(1)}, u32[]{:S(2)}, u32[]{:S(2)}) collective-permute-start(f32[4,4,8,128]{3,2,1,0:T(8,128)S(1)} %dynamic-slice_bitcast_fusion), channel_id=1, source_target_pairs={{0,1},{1,0},{2,3},{3,2},{4,5},{5,4},{6,7},{7,6},{8,9},{9,8},{10,11... | collective-permute-start | bytes 196616 | tf_op jit(solution)/shard_map/ppermute | solution.py:19

commit v3 on v2

v3 whole, which is shorter than its diff:
```python
import functools
import math

import jax
import jax.numpy as jnp
import ml_dtypes
from jax import lax
from jax.experimental import pallas as pl
from jax.experimental.pallas import tpu as pltpu
from jax.sharding import PartitionSpec as P

VMEM = pltpu.VMEM
LOG2E = math.log2(math.e)
HEIGHT = 16


def swapped(x, axis, mask):
    devices = lax.axis_size(axis)
    return lax.ppermute(x, axis, [(i, i ^ mask) for i in range(devices)])


def in_parts(scale):
    high = float(ml_dtypes.bfloat16(scale))
    return high, float(ml_dtypes.bfloat16(scale - high))


def stacked(pattern, parts):
    return jnp.concatenate(
        [jnp.where(pattern, part, 0.0).astype(jnp.bfloat16) for part in parts], axis=0
    )


def chunk_copies(chunk, density_ref, brick_ref, sem):
    half = brick_ref.shape[0] // 2
    copies = []
    for k in range(half // chunk):
        for first in (k * chunk, half + k * chunk):
            at = pl.ds(first, chunk)
            copies.append(
                pltpu.make_async_copy(density_ref.at[at], brick_ref.at[at], sem.at[len(copies)])
            )
    return copies


def totals_kernel(chunk, last, place_ref, density_ref, totals_ref, brick_ref, sem):
    cells, planes, lanes = brick_ref.shape
    half = cells // 2

    @pl.when(place_ref[0] == last)
    def _():
        totals_ref[...] = jnp.zeros_like(totals_ref)

    @pl.when(place_ref[0] != last)
    def _():
        copies = chunk_copies(chunk, density_ref, brick_ref, sem)
        for copy in copies:
            copy.start()
        row = lax.broadcasted_iota(jnp.int32, (16, 2 * lanes), 0)
        column = lax.broadcasted_iota(jnp.int32, (16, 2 * lanes), 1)
        pick = jnp.where(row == column // lanes, 1.0, 0.0).astype(jnp.bfloat16)

        def pair(v):
            return [brick_ref[v], brick_ref[half + v]]

        for k in range(half // chunk):
            copies[2 * k].wait()
            copies[2 * k + 1].wait()
            for v in range(k * chunk, (k + 1) * chunk, 4):
                left = jnp.concatenate(pair(v) + pair(v + 1), axis=0)
                right = jnp.concatenate(pair(v + 2) + pair(v + 3), axis=0)
                sums = lax.dot_general(
                    pick,
                    jnp.concatenate([left, right], axis=1),
                    (((1,), (1,)), ((), ())),
                    preferred_element_type=jnp.float32,
                )
                for j in range(4):
                    first = j % 2 * 2 * planes
                    totals_ref[v + j : v + j + 1] = sums[
                        j // 2 : j // 2 + 1, first : first + 2 * planes
                    ]


def brick_kernel(chunk, last, place_ref, density_ref, brick_in_ref, brick_ref, sem):
    @pl.when(place_ref[0] == last)
    def _():
        copies = chunk_copies(chunk, density_ref, brick_ref, sem)
        for copy in copies:
            copy.start()
        for copy in copies:
            copy.wait()


def local_kernel(
    rows,
    step_cells,
    light_parts,
    view_parts,
    place_ref,
    brick_ref,
    shade_ref,
    value_ref,
    still_ref,
    even,
    odd,
):
    cells, planes, lanes = brick_ref.shape
    chunks = cells // step_cells
    before = lax.broadcasted_iota(jnp.int32, (lanes, lanes), 0)
    after = lax.broadcasted_iota(jnp.int32, (lanes, lanes), 1)
    depths = jnp.concatenate(
        [stacked(before < after, light_parts), stacked(before == after, view_parts)], axis=1
    )

    def fill(chunk, at, buffer):
        packed = brick_ref[pl.ds(chunk * step_cells, step_cells), at]
        flat = packed.reshape(step_cells * rows, lanes)
        depth = jnp.dot(
            jnp.concatenate([flat, flat], axis=1), depths, preferred_element_type=jnp.float32
        )
        buffer[0] = jnp.exp2(depth[:, :lanes])
        buffer[1] = jnp.exp2(depth[:, lanes:])
        buffer[2] = depth[:, lanes:]

    def use(chunk, at, buffer, state, first):
        through, *moments = state
        for j in range(step_cells):
            cell = chunk * step_cells + j
            here = pl.ds(j * rows, rows)
            value = buffer[2, here]
            passed = through * buffer[1, here]
            weight = through - passed
            through = passed
            if first:
                weight = weight * (0.3 + buffer[0, here])
                moments[0] = moments[0] + weight
            else:
                value_ref[cell, at] = value
                shade_ref[cell, at] = weight * buffer[0, here]
            for i in (1, 2, 3):
                weight = weight * value
                moments[i] = moments[i] + weight
        return through, *moments

    def run(first):
        blocks = [pl.ds(z, rows) for z in range(0, planes, rows)]
        fill(0, blocks[0], even)
        for k, at in enumerate(blocks):
            zero = jnp.zeros((rows, lanes), jnp.float32)
            state = (jnp.ones((rows, lanes), jnp.float32), zero, zero, zero, zero)
            for chunk in range(0, chunks, 2):
                fill(chunk + 1, at, odd)
                state = use(chunk, at, even, state, first)
                if chunk + 2 < chunks:
                    fill(chunk + 2, at, even)
                elif k + 1 < len(blocks):
                    fill(0, blocks[k + 1], even)
                state = use(chunk + 1, at, odd, state, first)
            for i in range(5):
                still_ref[i, at] = state[i]

    @pl.when(place_ref[0] == 0)
    def _():
        run(True)

    @pl.when(place_ref[0] != 0)
    def _():
        run(False)


def lit_kernel(
    step_cells,
    light_scale,
    unit,
    place_ref,
    coef_ref,
    light_ref,
    still_ref,
    shade_ref,
    value_ref,
    out_ref,
    reach_ref,
    even,
    odd,
):
    cells, planes, lanes = shade_ref.shape
    blocks = planes // HEIGHT
    chunks = cells // step_cells
    def finish(k, moments):
        through = still_ref[0, pl.ds(k * HEIGHT, HEIGHT)]
        for c in range(3):
            out_ref[k, c] = (
                coef_ref[c, 0] * moments[0]
                + coef_ref[c, 1] * unit * moments[1]
                + coef_ref[c, 2] * unit**2 * moments[2]
                + coef_ref[c, 3] * unit**3 * moments[3]
            )
        out_ref[k, 3] = through

    pair = lax.broadcasted_iota(jnp.int32, (HEIGHT, cells), 1) // 2
    row = lax.broadcasted_iota(jnp.int32, (2 * cells, 2 * lanes), 0)
    column = lax.broadcasted_iota(jnp.int32, (2 * cells, 2 * lanes), 1)
    turns = jnp.where((row % 2 == 0) == (column < lanes), 1.0, 0.0).astype(jnp.bfloat16)

    def parts(k):
        reach = reach_ref[pl.ds(k * HEIGHT, HEIGHT)]
        high = reach.astype(jnp.bfloat16)
        return high, (reach - high.astype(jnp.float32)).astype(jnp.bfloat16)

    def fill(chunk, both, buffer):
        first = chunk * step_cells // 2
        picked = [
            jnp.concatenate([jnp.where(pair == first + p, part, 0) for part in both], axis=1)
            for p in range(step_cells // 2)
        ]
        spread = jnp.dot(
            jnp.concatenate(picked, axis=0), turns, preferred_element_type=jnp.float32
        )
        buffer[0] = spread[:, :lanes]
        buffer[1] = spread[:, lanes:]

    def use(chunk, k, buffer, state):
        m0, m1, m2, m3 = state
        at = pl.ds(k * HEIGHT, HEIGHT)
        for j in range(step_cells):
            cell = chunk * step_cells + j
            value = value_ref[cell, at]
            weight = shade_ref[cell, at] * buffer[j % 2, pl.ds(j // 2 * HEIGHT, HEIGHT)]
            m0 = m0 + weight
            weight = weight * value
            m1 = m1 + weight
            weight = weight * value
            m2 = m2 + weight
            weight = weight * value
            m3 = m3 + weight
        return m0, m1, m2, m3

    @pl.when(place_ref[0] == 0)
    def _():
        for k in range(blocks):
            finish(k, [still_ref[1 + i, pl.ds(k * HEIGHT, HEIGHT)] for i in range(4)])

    @pl.when(place_ref[0] != 0)
    def _():
        reach = jnp.exp2(light_ref[...] * light_scale).T
        half = reach.shape[0] // 2
        reach_ref[...] = jnp.concatenate([reach[:half], reach[half:]], axis=1)
        both = parts(0)
        fill(0, both, even)
        for k in range(blocks):
            state = (jnp.zeros((HEIGHT, lanes), jnp.float32),) * 4
            for chunk in range(0, chunks, 2):
                fill(chunk + 1, both, odd)
                state = use(chunk, k, even, state)
                if chunk + 2 < chunks:
                    fill(chunk + 2, both, even)
                elif k + 1 < blocks:
                    both = parts(k + 1)
                    fill(0, both, even)
                state = use(chunk + 1, k, odd, state)
            at = pl.ds(k * HEIGHT, HEIGHT)
            m0 = state[0] + 0.3 * (1.0 - still_ref[0, at])
            finish(k, [m0] + [state[i] + 0.3 * still_ref[1 + i, at] for i in (1, 2, 3)])


def over(pieces, order):
    total = 0.0
    for a, piece in enumerate(pieces):
        ahead = jnp.ones_like(piece[3])
        for b, other in enumerate(pieces):
            if a != b:
                ahead = ahead * jnp.where(order[b] < order[a], other[3], 1.0)
        total = total + piece[:3] * ahead[None]
    return total


def body(density, color_coef):
    cells, planes, lanes = density.shape
    light_count = lax.axis_size("light")
    view_count = lax.axis_size("view")
    light_scale = -2.0 / (lanes * light_count) * LOG2E
    view_parts = in_parts(-2.0 / (cells * view_count) * LOG2E)
    own_rows = planes // view_count
    chunk = 32
    step_cells = 16
    rows = 32
    lit_cells = 16
    whole = pl.BlockSpec(memory_space=VMEM)
    scalars = pl.BlockSpec(memory_space=pltpu.SMEM)

    place = lax.axis_index("light")
    where = place.astype(jnp.int32)[None]
    brick_shape = jax.ShapeDtypeStruct(density.shape, density.dtype)
    sem = pltpu.SemaphoreType.DMA((cells // chunk,))
    wide = pltpu.CompilerParams(vmem_limit_bytes=50 * 2**20 + 2**19)
    totals, brick = pl.pallas_call(
        functools.partial(totals_kernel, chunk, light_count - 1),
        name="totals_kernel",
        out_shape=[jax.ShapeDtypeStruct((cells // 2, 2 * planes), jnp.float32), brick_shape],
        in_specs=[scalars, pl.BlockSpec(memory_space=pltpu.HBM)],
        out_specs=[whole, whole],
        scratch_shapes=[sem],
        compiler_params=wide,
    )(where, density)

    arrived = [(mask, swapped(totals, "light", mask)) for mask in range(light_count - 1, 0, -1)]

    brick = pl.pallas_call(
        functools.partial(brick_kernel, chunk, light_count - 1),
        name="brick_kernel",
        out_shape=brick_shape,
        in_specs=[scalars, pl.BlockSpec(memory_space=pltpu.HBM), whole],
        out_specs=whole,
        input_output_aliases={2: 0},
        scratch_shapes=[sem],
        compiler_params=wide,
    )(where, density, brick)

    mine = lax.axis_index("view")
    core, chip = mine % 2, mine // 2
    chips = view_count // 2
    others = list(range(chips - 1, 0, -1))
    table = jax.ShapeDtypeStruct(density.shape, jnp.float32)
    shade, value, still = pl.pallas_call(
        functools.partial(local_kernel, rows, step_cells, in_parts(light_scale), view_parts),
        name="local_kernel",
        out_shape=[table, table, jax.ShapeDtypeStruct((5, planes, lanes), jnp.float32)],
        in_specs=[scalars, whole],
        out_specs=[whole] * 3,
        scratch_shapes=[VMEM((3, step_cells * rows, lanes), jnp.float32)] * 2,
        compiler_params=pltpu.CompilerParams(vmem_limit_bytes=8 * 2**20),
        cost_estimate=pl.CostEstimate(
            flops=20 * density.size, bytes_accessed=2**23, transcendentals=2 * density.size
        ),
    )(where, brick)

    upstream = jnp.zeros_like(totals)
    for mask, other in arrived:
        upstream = upstream + jnp.where(place ^ mask < place, other, 0.0)

    away = pl.pallas_call(
        functools.partial(lit_kernel, lit_cells, light_scale, 1.0 / sum(view_parts)),
        name="lit_kernel",
        out_shape=jax.ShapeDtypeStruct((planes // HEIGHT, 4, HEIGHT, lanes), jnp.float32),
        in_specs=[scalars] * 2 + [whole] * 4,
        out_specs=whole,
        scratch_shapes=[VMEM((planes, cells), jnp.float32)]
        + [VMEM((2, lit_cells // 2 * HEIGHT, lanes), jnp.float32)] * 2,
        compiler_params=pltpu.CompilerParams(vmem_limit_bytes=8 * 2**20),
    )(where, color_coef, upstream, still, shade, value)

    if 2 * own_rows != HEIGHT:
        away = jnp.swapaxes(away, 0, 1).reshape(4, chips, 2 * own_rows, lanes)
        away = jnp.swapaxes(away, 0, 1)
    sent = [lax.dynamic_index_in_dim(away, chip ^ mask, 0, False) for mask in others]
    own = lax.dynamic_index_in_dim(away, chip, 0, False)
    pieces = [own] + [swapped(x, "view", 2 * mask) for x, mask in zip(sent, others)]
    order = [chip] + [chip ^ mask for mask in others]
    pieces = jnp.stack(pieces).reshape(chips, 4, 2, own_rows, lanes)
    keep = lax.dynamic_index_in_dim(pieces, core, 2, False)
    took = swapped(lax.dynamic_index_in_dim(pieces, 1 - core, 2, False), "view", 1)
    near = jnp.where(core == 0, keep, took)
    far = jnp.where(core == 0, took, keep)
    color = near[:, :3] + near[:, 3:] * far[:, :3]
    both = jnp.concatenate([color, near[:, 3:] * far[:, 3:]], axis=1)
    return over([both[k] for k in range(chips)], order)


def solution(mesh):
    placed = (P("view", None, "light"), P())
    return jax.shard_map(
        body, mesh=mesh, in_specs=placed, out_specs=P(None, "view", "light"), check_vma=False
    )
```

time: 23.5 us -> 20.8 us (0.89)
  the two profiles are of different devices: /device:TPU:0 before, /device:TPU:9 now
where the time goes in v3:
time: 20.8 us; the launch traced here: 20.6 us
  starting transfers between devices  9.22 us (44%)
  Pallas kernels  7.1 us (34%)
  waiting for transfers between devices  3.42 us (16%)
  other arithmetic  0.69 us (3%)
    ppermute x7, starting transfers between devices, swapped(): return lax.ppermute(x, axis, [(i, i ^ mask) for i in range(devices)])  9.22 us
    ppermute x7, waiting for transfers between devices, swapped(): return lax.ppermute(x, axis, [(i, i ^ mask) for i in range(devices)])  3.42 us
    pallas_call x1, Pallas kernels, body(): pl.pallas_call(functools.partial(local_kernel, rows, step_cells, in_parts...  2.61 us
    pallas_call x1, Pallas kernels, body(): pl.pallas_call(functools.partial(lit_kernel, lit_cells, light_scale, 1.0...  2.45 us
    pallas_call x1, Pallas kernels, body(): pl.pallas_call(functools.partial(totals_kernel, chunk, light_count - 1),...  2.01 us
    add x1, other arithmetic, over(): total = total + piece[:3] * ahead[None]  0.61 us
  transfers between devices with their start and end apart: 7, of which 4 were waited for; matrix products, arithmetic and copies ran while one was open for 0% of the time, Pallas kernels for 13%

profile of v3, /device:TPU:9, one launch (start us, length us, event | category | flops | bytes accessed | tf_op | source)
XLA Modules:
  0.0 20.6 jit_solution(3217451107989408833)
XLA Ops:
  0.0 2.0 %totals_kernel.1 = (f32[64,128]{1,0:T(8,128)S(1)}, bf16[128,64,128]{2,1,0:T(8,128)(2,1)S(1)}) custom-call(s32[1]{0:T(128)} %bitcast.place_ref, bf16[128,64,128]{2,1,0:T(8,128)(2,1)} %density_ref.3), custom_call_target="tpu_custom_call" | custom-call | tf_op jit(solution)/shard_map/totals_kernel/pallas_call | solution.py:296
  2.0 1.4 %collective-permute-start = (f32[64,128]{1,0:T(8,128)S(1)}, f32[64,128]{1,0:T(8,128)S(1)}, u32[]{:S(2)}, u32[]{:S(2)}) collective-permute-start(f32[64,128]{1,0:T(8,128)S(1)} %get-tuple-element.10), channel_id=1, source_target_pairs={{0,24},{8,16},{16,8},{24,0},{1,25},{9,17},{17,9},{25,1},{2,26},{10... | collective-permute-start | bytes 98312 | tf_op jit(solution)/shard_map/ppermute | solution.py:19
  3.4 0.1 collective-permute-start.1
  3.5 1.2 %collective-permute-start.2 = (f32[64,128]{1,0:T(8,128)S(1)}, f32[64,128]{1,0:T(8,128)S(1)}, u32[]{:S(2)}, u32[]{:S(2)}) collective-permute-start(f32[64,128]{1,0:T(8,128)S(1)} %get-tuple-element.10), channel_id=1, source_target_pairs={{0,8},{8,0},{16,24},{24,16},{1,9},{9,1},{17,25},{25,17},{2,10},{10... | collective-permute-start | bytes 98312 | tf_op jit(solution)/shard_map/ppermute | solution.py:19
  4.8 0.0 copy-start
  4.8 2.6 %local_kernel.1 = (f32[128,64,128]{2,1,0:T(8,128)S(1)}, f32[128,64,128]{2,1,0:T(8,128)S(1)}, f32[5,64,128]{2,1,0:T(8,128)S(1)}) custom-call(s32[1]{0:T(128)} %bitcast.place_ref, bf16[128,64,128]{2,1,0:T(8,128)(2,1)S(1)} %brick_kernel.1.brick_ref), custom_call_target="tpu_custom_call" | custom-call | flops 20971520 | bytes 8388608 | tf_op jit(solution)/shard_map/local_kernel/pallas_call | solution.py:324
  7.4 0.0 collective-permute-done
  7.4 0.0 collective-permute-done.1
  7.4 0.0 collective-permute-done.2
  7.5 0.0 copy-done
  7.5 2.4 %lit_kernel.1 = f32[4,4,16,128]{3,2,1,0:T(8,128)S(1)} custom-call(s32[1]{0:T(128)} %bitcast.place_ref, f32[3,4]{1,0:T(4,128)S(1)} %copy-done, f32[64,128]{1,0:T(8,128)S(1)} %select_add_fusion.light_ref, f32[5,64,128]{2,1,0:T(8,128)S(1)} %get-tuple-element.12.still_ref, f32[128,64,128]{2,1,0:T(8,128)S(1)} %get-tuple-element.13.shade_ref, ...), custom_call_target="tpu_custom_call" | custom-call | tf_op jit(solution)/shard_map/lit_kernel/pallas_call | solution.py:341
  10.0 2.2 %collective-permute-start.3 = (f32[4,16,128]{2,1,0:T(8,128)S(1)}, f32[4,16,128]{2,1,0:T(8,128)S(1)}, u32[]{:S(2)}, u32[]{:S(2)}) collective-permute-start(f32[4,16,128]{2,1,0:T(8,128)S(1)} %get-tuple-element.20), channel_id=1, source_target_pairs={{0,6},{1,7},{2,4},{3,5},{4,2},{5,3},{6,0},{7,1},{8,14},{9,15},{10,... | collective-permute-start | bytes 98312 | tf_op jit(solution)/shard_map/ppermute | solution.py:19
  12.2 0.2 %collective-permute-start.4 = (f32[4,16,128]{2,1,0:T(8,128)S(1)}, f32[4,16,128]{2,1,0:T(8,128)S(1)}, u32[]{:S(2)}, u32[]{:S(2)}) collective-permute-start(f32[4,16,128]{2,1,0:T(8,128)S(1)} %get-tuple-element.19), channel_id=1, source_target_pairs={{0,4},{1,5},{2,6},{3,7},{4,0},{5,1},{6,2},{7,3},{8,12},{9,13},{10,... | collective-permute-start | bytes 98312 | tf_op jit(solution)/shard_map/ppermute | solution.py:19
  12.4 0.3 %collective-permute-start.5 = (f32[4,16,128]{2,1,0:T(8,128)S(1)}, f32[4,16,128]{2,1,0:T(8,128)S(1)}, u32[]{:S(2)}, u32[]{:S(2)}) collective-permute-start(f32[4,16,128]{2,1,0:T(8,128)S(1)} %get-tuple-element.18), channel_id=1, source_target_pairs={{0,2},{1,3},{2,0},{3,1},{4,6},{5,7},{6,4},{7,5},{8,10},{9,11},{10,... | collective-permute-start | bytes 98312 | tf_op jit(solution)/shard_map/ppermute | solution.py:19
  12.7 1.0 %collective-permute-done.3 = f32[4,16,128]{2,1,0:T(8,128)S(1)} collective-permute-done((f32[4,16,128]{2,1,0:T(8,128)S(1)}, f32[4,16,128]{2,1,0:T(8,128)S(1)}, u32[]{:S(2)}, u32[]{:S(2)}) %collective-permute-start.3) | collective-permute-done | bytes 32800 | tf_op jit(solution)/shard_map/ppermute | solution.py:19
  13.7 1.3 %collective-permute-done.4 = f32[4,16,128]{2,1,0:T(8,128)S(1)} collective-permute-done((f32[4,16,128]{2,1,0:T(8,128)S(1)}, f32[4,16,128]{2,1,0:T(8,128)S(1)}, u32[]{:S(2)}, u32[]{:S(2)}) %collective-permute-start.4) | collective-permute-done | bytes 32800 | tf_op jit(solution)/shard_map/ppermute | solution.py:19
  15.0 0.2 %collective-permute-done.5 = f32[4,16,128]{2,1,0:T(8,128)S(1)} collective-permute-done((f32[4,16,128]{2,1,0:T(8,128)S(1)}, f32[4,16,128]{2,1,0:T(8,128)S(1)}, u32[]{:S(2)}, u32[]{:S(2)}) %collective-permute-start.5) | collective-permute-done | bytes 32800 | tf_op jit(solution)/shard_map/ppermute | solution.py:19
  15.2 3.8 %collective-permute-start.6 = (f32[4,4,8,128]{3,2,1,0:T(8,128)S(1)}, f32[4,4,8,128]{3,2,1,0:T(8,128)S(1)}, u32[]{:S(2)}, u32[]{:S(2)}) collective-permute-start(f32[4,4,8,128]{3,2,1,0:T(8,128)S(1)} %dynamic-slice_bitcast_fusion), channel_id=1, source_target_pairs={{0,1},{1,0},{2,3},{3,2},{4,5},{5,4},{6,7},{7,6},{8,9},{9,8},{10,11... | collective-permute-start | bytes 196616 | tf_op jit(solution)/shard_map/ppermute | solution.py:19
  19.0 0.9 %collective-permute-done.6 = f32[4,4,8,128]{3,2,1,0:T(8,128)S(1)} collective-permute-done((f32[4,4,8,128]{3,2,1,0:T(8,128)S(1)}, f32[4,4,8,128]{3,2,1,0:T(8,128)S(1)}, u32[]{:S(2)}, u32[]{:S(2)}) %collective-permute-start.6) | collective-permute-done | bytes 65568 | tf_op jit(solution)/shard_map/ppermute | solution.py:19
  20.0 0.6 %fusion.2 = f32[3,8,128]{2,1,0:T(8,128)} fusion(f32[4,3,8,128]{3,2,1,0:T(8,128)S(1)} %fusion, f32[8,128]{1,0:T(8,128)S(1)} %multiply_bitcast_fusion, f32[8,128]{1,0:T(8,128)S(1)} %get-tuple-element.25, f32[8,128]{1,0:T(8,128)S(1)} %get-tuple-element.24, f32[8,128]{1,0:T(8,128)S(1)} %get-tuple-element.23), kind=kLoop, calls=%fused_computation.15 | loop fusion | flops 21504 | bytes 77824 | tf_op jit(solution)/shard_map/add | solution.py:273
  (10 shorter events, 0.2 us)
Async XLA Ops:
  2.0 5.4 %collective-permute-start = (f32[64,128]{1,0:T(8,128)S(1)}, f32[64,128]{1,0:T(8,128)S(1)}, u32[]{:S(2)}, u32[]{:S(2)}) collective-permute-start(f32[64,128]{1,0:T(8,128)S(1)} %get-tuple-element.10), channel_id=1, source_target_pairs={{0,24},{8,16},{16,8},{24,0},{1,25},{9,17},{17,9},{25,1},{2,26},{10... | collective-permute-start | bytes 98312 | tf_op jit(solution)/shard_map/ppermute | solution.py:19
  3.4 4.1 %collective-permute-start.1 = (f32[64,128]{1,0:T(8,128)S(1)}, f32[64,128]{1,0:T(8,128)S(1)}, u32[]{:S(2)}, u32[]{:S(2)}) collective-permute-start(f32[64,128]{1,0:T(8,128)S(1)} %get-tuple-element.10), channel_id=1, source_target_pairs={{0,16},{8,24},{16,0},{24,8},{1,17},{9,25},{17,1},{25,9},{2,18},{10... | collective-permute-start | bytes 98312 | tf_op jit(solution)/shard_map/ppermute | solution.py:19
  3.5 3.9 %collective-permute-start.2 = (f32[64,128]{1,0:T(8,128)S(1)}, f32[64,128]{1,0:T(8,128)S(1)}, u32[]{:S(2)}, u32[]{:S(2)}) collective-permute-start(f32[64,128]{1,0:T(8,128)S(1)} %get-tuple-element.10), channel_id=1, source_target_pairs={{0,8},{8,0},{16,24},{24,16},{1,9},{9,1},{17,25},{25,17},{2,10},{10... | collective-permute-start | bytes 98312 | tf_op jit(solution)/shard_map/ppermute | solution.py:19
  4.8 2.7 %copy-start = (f32[3,4]{1,0:T(4,128)S(1)}, f32[3,4]{1,0:T(4,128)}, u32[]{:S(2)}) copy-start(f32[3,4]{1,0:T(4,128)} %coef_ref.1) | copy-start | bytes 148
  10.0 3.7 %collective-permute-start.3 = (f32[4,16,128]{2,1,0:T(8,128)S(1)}, f32[4,16,128]{2,1,0:T(8,128)S(1)}, u32[]{:S(2)}, u32[]{:S(2)}) collective-permute-start(f32[4,16,128]{2,1,0:T(8,128)S(1)} %get-tuple-element.20), channel_id=1, source_target_pairs={{0,6},{1,7},{2,4},{3,5},{4,2},{5,3},{6,0},{7,1},{8,14},{9,15},{10,... | collective-permute-start | bytes 98312 | tf_op jit(solution)/shard_map/ppermute | solution.py:19
  12.2 2.8 %collective-permute-start.4 = (f32[4,16,128]{2,1,0:T(8,128)S(1)}, f32[4,16,128]{2,1,0:T(8,128)S(1)}, u32[]{:S(2)}, u32[]{:S(2)}) collective-permute-start(f32[4,16,128]{2,1,0:T(8,128)S(1)} %get-tuple-element.19), channel_id=1, source_target_pairs={{0,4},{1,5},{2,6},{3,7},{4,0},{5,1},{6,2},{7,3},{8,12},{9,13},{10,... | collective-permute-start | bytes 98312 | tf_op jit(solution)/shard_map/ppermute | solution.py:19
  12.4 2.8 %collective-permute-start.5 = (f32[4,16,128]{2,1,0:T(8,128)S(1)}, f32[4,16,128]{2,1,0:T(8,128)S(1)}, u32[]{:S(2)}, u32[]{:S(2)}) collective-permute-start(f32[4,16,128]{2,1,0:T(8,128)S(1)} %get-tuple-element.18), channel_id=1, source_target_pairs={{0,2},{1,3},{2,0},{3,1},{4,6},{5,7},{6,4},{7,5},{8,10},{9,11},{10,... | collective-permute-start | bytes 98312 | tf_op jit(solution)/shard_map/ppermute | solution.py:19
  15.2 4.7 %collective-permute-start.6 = (f32[4,4,8,128]{3,2,1,0:T(8,128)S(1)}, f32[4,4,8,128]{3,2,1,0:T(8,128)S(1)}, u32[]{:S(2)}, u32[]{:S(2)}) collective-permute-start(f32[4,4,8,128]{3,2,1,0:T(8,128)S(1)} %dynamic-slice_bitcast_fusion), channel_id=1, source_target_pairs={{0,1},{1,0},{2,3},{3,2},{4,5},{5,4},{6,7},{7,6},{8,9},{9,8},{10,11... | collective-permute-start | bytes 196616 | tf_op jit(solution)/shard_map/ppermute | solution.py:19

commit v4 on v3

--- a/solution.py
+++ b/solution.py
@@ -101,8 +101,6 @@
     shade_ref,
     value_ref,
     still_ref,
-    even,
-    odd,
 ):
     cells, planes, lanes = brick_ref.shape
     chunks = cells // step_cells
@@ -112,31 +110,28 @@
         [stacked(before < after, light_parts), stacked(before == after, view_parts)], axis=1
     )
 
-    def fill(chunk, at, buffer):
+    def fill(chunk, at):
         packed = brick_ref[pl.ds(chunk * step_cells, step_cells), at]
         flat = packed.reshape(step_cells * rows, lanes)
         depth = jnp.dot(
             jnp.concatenate([flat, flat], axis=1), depths, preferred_element_type=jnp.float32
         )
-        buffer[0] = jnp.exp2(depth[:, :lanes])
-        buffer[1] = jnp.exp2(depth[:, lanes:])
-        buffer[2] = depth[:, lanes:]
+        return jnp.exp2(depth[:, :lanes]), jnp.exp2(depth[:, lanes:]), depth[:, lanes:]
 
     def use(chunk, at, buffer, state, first):
         through, *moments = state
         for j in range(step_cells):
             cell = chunk * step_cells + j
-            here = pl.ds(j * rows, rows)
-            value = buffer[2, here]
-            passed = through * buffer[1, here]
+            lit, pass_on, value = (x[j * rows : (j + 1) * rows] for x in buffer)
+            passed = through * pass_on
             weight = through - passed
             through = passed
             if first:
-                weight = weight * (0.3 + buffer[0, here])
+                weight = weight * (0.3 + lit)
                 moments[0] = moments[0] + weight
             else:
                 value_ref[cell, at] = value
-                shade_ref[cell, at] = weight * buffer[0, here]
+                shade_ref[cell, at] = weight * lit
             for i in (1, 2, 3):
                 weight = weight * value
                 moments[i] = moments[i] + weight
@@ -144,18 +139,11 @@
 
     def run(first):
         blocks = [pl.ds(z, rows) for z in range(0, planes, rows)]
-        fill(0, blocks[0], even)
         for k, at in enumerate(blocks):
             zero = jnp.zeros((rows, lanes), jnp.float32)
             state = (jnp.ones((rows, lanes), jnp.float32), zero, zero, zero, zero)
-            for chunk in range(0, chunks, 2):
-                fill(chunk + 1, at, odd)
-                state = use(chunk, at, even, state, first)
-                if chunk + 2 < chunks:
-                    fill(chunk + 2, at, even)
-                elif k + 1 < len(blocks):
-                    fill(0, blocks[k + 1], even)
-                state = use(chunk + 1, at, odd, state, first)
+            for chunk in range(chunks):
+                state = use(chunk, at, fill(chunk, at), state, first)
             for i in range(5):
                 still_ref[i, at] = state[i]
 
@@ -180,34 +168,27 @@
     value_ref,
     out_ref,
     reach_ref,
-    even,
-    odd,
 ):
     cells, planes, lanes = shade_ref.shape
     blocks = planes // HEIGHT
     chunks = cells // step_cells
+    def block_rows(k):
+        return pl.ds(k * HEIGHT if isinstance(k, int) else pl.multiple_of(k * HEIGHT, HEIGHT), HEIGHT)
+
     def finish(k, moments):
-        through = still_ref[0, pl.ds(k * HEIGHT, HEIGHT)]
+        through = still_ref[0, block_rows(k)]
         for c in range(3):
-            out_ref[k, c] = (
-                coef_ref[c, 0] * moments[0]
-                + coef_ref[c, 1] * unit * moments[1]
-                + coef_ref[c, 2] * unit**2 * moments[2]
-                + coef_ref[c, 3] * unit**3 * moments[3]
+            out_ref[k, c] = sum(
+                coef_ref[c : c + 1, i : i + 1] * unit**i * moments[i] for i in range(4)
             )
         out_ref[k, 3] = through
 
-    pair = lax.broadcasted_iota(jnp.int32, (HEIGHT, cells), 1) // 2
-    row = lax.broadcasted_iota(jnp.int32, (2 * cells, 2 * lanes), 0)
-    column = lax.broadcasted_iota(jnp.int32, (2 * cells, 2 * lanes), 1)
-    turns = jnp.where((row % 2 == 0) == (column < lanes), 1.0, 0.0).astype(jnp.bfloat16)
-
     def parts(k):
-        reach = reach_ref[pl.ds(k * HEIGHT, HEIGHT)]
+        reach = reach_ref[block_rows(k)]
         high = reach.astype(jnp.bfloat16)
         return high, (reach - high.astype(jnp.float32)).astype(jnp.bfloat16)
 
-    def fill(chunk, both, buffer):
+    def fill(chunk, both, pair, turns):
         first = chunk * step_cells // 2
         picked = [
             jnp.concatenate([jnp.where(pair == first + p, part, 0) for part in both], axis=1)
@@ -216,16 +197,16 @@
         spread = jnp.dot(
             jnp.concatenate(picked, axis=0), turns, preferred_element_type=jnp.float32
         )
-        buffer[0] = spread[:, :lanes]
-        buffer[1] = spread[:, lanes:]
-
-    def use(chunk, k, buffer, state):
+        return spread[:, :lanes], spread[:, lanes:]
+
+    def use(chunk, k, spread, state):
         m0, m1, m2, m3 = state
-        at = pl.ds(k * HEIGHT, HEIGHT)
+        at = block_rows(k)
         for j in range(step_cells):
             cell = chunk * step_cells + j
             value = value_ref[cell, at]
-            weight = shade_ref[cell, at] * buffer[j % 2, pl.ds(j // 2 * HEIGHT, HEIGHT)]
+            here = slice(j // 2 * HEIGHT, (j // 2 + 1) * HEIGHT)
+            weight = shade_ref[cell, at] * spread[j % 2][here]
             m0 = m0 + weight
             weight = weight * value
             m1 = m1 + weight
@@ -238,27 +219,23 @@
     @pl.when(place_ref[0] == 0)
     def _():
         for k in range(blocks):
-            finish(k, [still_ref[1 + i, pl.ds(k * HEIGHT, HEIGHT)] for i in range(4)])
+            finish(k, [still_ref[1 + i, block_rows(k)] for i in range(4)])
 
     @pl.when(place_ref[0] != 0)
     def _():
+        pair = lax.broadcasted_iota(jnp.int32, (HEIGHT, cells), 1) // 2
+        row = lax.broadcasted_iota(jnp.int32, (2 * cells, 2 * lanes), 0)
+        column = lax.broadcasted_iota(jnp.int32, (2 * cells, 2 * lanes), 1)
+        turns = jnp.where((row % 2 == 0) == (column < lanes), 1.0, 0.0).astype(jnp.bfloat16)
         reach = jnp.exp2(light_ref[...] * light_scale).T
         half = reach.shape[0] // 2
         reach_ref[...] = jnp.concatenate([reach[:half], reach[half:]], axis=1)
-        both = parts(0)
-        fill(0, both, even)
         for k in range(blocks):
+            both = parts(k)
             state = (jnp.zeros((HEIGHT, lanes), jnp.float32),) * 4
-            for chunk in range(0, chunks, 2):
-                fill(chunk + 1, both, odd)
-                state = use(chunk, k, even, state)
-                if chunk + 2 < chunks:
-                    fill(chunk + 2, both, even)
-                elif k + 1 < blocks:
-                    both = parts(k + 1)
-                    fill(0, both, even)
-                state = use(chunk + 1, k, odd, state)
-            at = pl.ds(k * HEIGHT, HEIGHT)
+            for chunk in range(chunks):
+                state = use(chunk, k, fill(chunk, both, pair, turns), state)
+            at = block_rows(k)
             m0 = state[0] + 0.3 * (1.0 - still_ref[0, at])
             finish(k, [m0] + [state[i] + 0.3 * still_ref[1 + i, at] for i in (1, 2, 3)])
 
@@ -282,9 +259,9 @@
     view_parts = in_parts(-2.0 / (cells * view_count) * LOG2E)
     own_rows = planes // view_count
     chunk = 32
-    step_cells = 16
-    rows = 32
-    lit_cells = 16
+    step_cells = 32
+    rows = 16
+    lit_cells = 32
     whole = pl.BlockSpec(memory_space=VMEM)
     scalars = pl.BlockSpec(memory_space=pltpu.SMEM)
 
@@ -327,7 +304,6 @@
         out_shape=[table, table, jax.ShapeDtypeStruct((5, planes, lanes), jnp.float32)],
         in_specs=[scalars, whole],
         out_specs=[whole] * 3,
-        scratch_shapes=[VMEM((3, step_cells * rows, lanes), jnp.float32)] * 2,
         compiler_params=pltpu.CompilerParams(vmem_limit_bytes=8 * 2**20),
         cost_estimate=pl.CostEstimate(
             flops=20 * density.size, bytes_accessed=2**23, transcendentals=2 * density.size
@@ -342,10 +318,9 @@
         functools.partial(lit_kernel, lit_cells, light_scale, 1.0 / sum(view_parts)),
         name="lit_kernel",
         out_shape=jax.ShapeDtypeStruct((planes // HEIGHT, 4, HEIGHT, lanes), jnp.float32),
-        in_specs=[scalars] * 2 + [whole] * 4,
+        in_specs=[scalars] + [whole] * 5,
         out_specs=whole,
-        scratch_shapes=[VMEM((planes, cells), jnp.float32)]
-        + [VMEM((2, lit_cells // 2 * HEIGHT, lanes), jnp.float32)] * 2,
+        scratch_shapes=[VMEM((planes, cells), jnp.float32)],
         compiler_params=pltpu.CompilerParams(vmem_limit_bytes=8 * 2**20),
     )(where, color_coef, upstream, still, shade, value)
 

time: 20.8 us -> 20.2 us (0.971)
  the two profiles are of different devices: /device:TPU:9 before, /device:TPU:13 now
where the time goes in v4:
time: 20.2 us; the launch traced here: 20.1 us
  starting transfers between devices  9.26 us (46%)
  Pallas kernels  6.16 us (30%)
  waiting for transfers between devices  3.79 us (19%)
  other arithmetic  0.68 us (3%)
    ppermute x7, starting transfers between devices, swapped(): return lax.ppermute(x, axis, [(i, i ^ mask) for i in range(devices)])  9.26 us
    ppermute x7, waiting for transfers between devices, swapped(): return lax.ppermute(x, axis, [(i, i ^ mask) for i in range(devices)])  3.79 us
    pallas_call x1, Pallas kernels, body(): pl.pallas_call(functools.partial(local_kernel, rows, step_cells, in_parts...  2.23 us
    pallas_call x1, Pallas kernels, body(): pl.pallas_call(functools.partial(totals_kernel, chunk, light_count - 1),...  2.01 us
    pallas_call x1, Pallas kernels, body(): pl.pallas_call(functools.partial(lit_kernel, lit_cells, light_scale, 1.0...  1.88 us
    add x1, other arithmetic, over(): total = total + piece[:3] * ahead[None]  0.61 us
  transfers between devices with their start and end apart: 7, of which 5 were waited for; matrix products, arithmetic and copies ran while one was open for 0% of the time, Pallas kernels for 11%

profile of v4, /device:TPU:13, one launch (start us, length us, event | category | flops | bytes accessed | tf_op | source)
XLA Modules:
  0.0 20.1 jit_solution(4706656770955723405)
XLA Ops:
  0.0 2.0 %totals_kernel.1 = (f32[64,128]{1,0:T(8,128)S(1)}, bf16[128,64,128]{2,1,0:T(8,128)(2,1)S(1)}) custom-call(s32[1]{0:T(128)} %bitcast.place_ref, bf16[128,64,128]{2,1,0:T(8,128)(2,1)} %density_ref.3), custom_call_target="tpu_custom_call" | custom-call | tf_op jit(solution)/shard_map/totals_kernel/pallas_call | solution.py:273
  2.0 1.4 %collective-permute-start = (f32[64,128]{1,0:T(8,128)S(1)}, f32[64,128]{1,0:T(8,128)S(1)}, u32[]{:S(2)}, u32[]{:S(2)}) collective-permute-start(f32[64,128]{1,0:T(8,128)S(1)} %get-tuple-element.10), channel_id=1, source_target_pairs={{0,24},{8,16},{16,8},{24,0},{1,25},{9,17},{17,9},{25,1},{2,26},{10... | collective-permute-start | bytes 98312 | tf_op jit(solution)/shard_map/ppermute | solution.py:19
  3.4 1.0 %collective-permute-start.1 = (f32[64,128]{1,0:T(8,128)S(1)}, f32[64,128]{1,0:T(8,128)S(1)}, u32[]{:S(2)}, u32[]{:S(2)}) collective-permute-start(f32[64,128]{1,0:T(8,128)S(1)} %get-tuple-element.10), channel_id=1, source_target_pairs={{0,16},{8,24},{16,0},{24,8},{1,17},{9,25},{17,1},{25,9},{2,18},{10... | collective-permute-start | bytes 98312 | tf_op jit(solution)/shard_map/ppermute | solution.py:19
  4.3 0.4 %collective-permute-start.2 = (f32[64,128]{1,0:T(8,128)S(1)}, f32[64,128]{1,0:T(8,128)S(1)}, u32[]{:S(2)}, u32[]{:S(2)}) collective-permute-start(f32[64,128]{1,0:T(8,128)S(1)} %get-tuple-element.10), channel_id=1, source_target_pairs={{0,8},{8,0},{16,24},{24,16},{1,9},{9,1},{17,25},{25,17},{2,10},{10... | collective-permute-start | bytes 98312 | tf_op jit(solution)/shard_map/ppermute | solution.py:19
  4.8 0.0 copy-start
  4.8 2.2 %local_kernel.1 = (f32[128,64,128]{2,1,0:T(8,128)S(1)}, f32[128,64,128]{2,1,0:T(8,128)S(1)}, f32[5,64,128]{2,1,0:T(8,128)S(1)}) custom-call(s32[1]{0:T(128)} %bitcast.place_ref, bf16[128,64,128]{2,1,0:T(8,128)(2,1)S(1)} %brick_kernel.1.brick_ref), custom_call_target="tpu_custom_call" | custom-call | flops 20971520 | bytes 8388608 | tf_op jit(solution)/shard_map/local_kernel/pallas_call | solution.py:301
  7.0 0.0 collective-permute-done
  7.1 0.1 collective-permute-done.1
  7.1 0.0 collective-permute-done.2
  7.1 0.0 copy-done
  7.2 1.9 %lit_kernel.1 = f32[4,4,16,128]{3,2,1,0:T(8,128)S(1)} custom-call(s32[1]{0:T(128)} %bitcast.place_ref, f32[3,4]{1,0:T(4,128)S(1)} %copy-done, f32[64,128]{1,0:T(8,128)S(1)} %select_add_fusion.light_ref, f32[5,64,128]{2,1,0:T(8,128)S(1)} %get-tuple-element.12.still_ref, f32[128,64,128]{2,1,0:T(8,128)S(1)} %get-tuple-element.13.shade_ref, ...), custom_call_target="tpu_custom_call" | custom-call | tf_op jit(solution)/shard_map/lit_kernel/pallas_call | solution.py:317
  9.1 1.2 %collective-permute-start.3 = (f32[4,16,128]{2,1,0:T(8,128)S(1)}, f32[4,16,128]{2,1,0:T(8,128)S(1)}, u32[]{:S(2)}, u32[]{:S(2)}) collective-permute-start(f32[4,16,128]{2,1,0:T(8,128)S(1)} %get-tuple-element.20), channel_id=1, source_target_pairs={{0,6},{1,7},{2,4},{3,5},{4,2},{5,3},{6,0},{7,1},{8,14},{9,15},{10,... | collective-permute-start | bytes 98312 | tf_op jit(solution)/shard_map/ppermute | solution.py:19
  10.3 1.2 %collective-permute-start.4 = (f32[4,16,128]{2,1,0:T(8,128)S(1)}, f32[4,16,128]{2,1,0:T(8,128)S(1)}, u32[]{:S(2)}, u32[]{:S(2)}) collective-permute-start(f32[4,16,128]{2,1,0:T(8,128)S(1)} %get-tuple-element.19), channel_id=1, source_target_pairs={{0,4},{1,5},{2,6},{3,7},{4,0},{5,1},{6,2},{7,3},{8,12},{9,13},{10,... | collective-permute-start | bytes 98312 | tf_op jit(solution)/shard_map/ppermute | solution.py:19
  11.5 0.3 %collective-permute-start.5 = (f32[4,16,128]{2,1,0:T(8,128)S(1)}, f32[4,16,128]{2,1,0:T(8,128)S(1)}, u32[]{:S(2)}, u32[]{:S(2)}) collective-permute-start(f32[4,16,128]{2,1,0:T(8,128)S(1)} %get-tuple-element.18), channel_id=1, source_target_pairs={{0,2},{1,3},{2,0},{3,1},{4,6},{5,7},{6,4},{7,5},{8,10},{9,11},{10,... | collective-permute-start | bytes 98312 | tf_op jit(solution)/shard_map/ppermute | solution.py:19
  11.8 1.0 %collective-permute-done.3 = f32[4,16,128]{2,1,0:T(8,128)S(1)} collective-permute-done((f32[4,16,128]{2,1,0:T(8,128)S(1)}, f32[4,16,128]{2,1,0:T(8,128)S(1)}, u32[]{:S(2)}, u32[]{:S(2)}) %collective-permute-start.3) | collective-permute-done | bytes 32800 | tf_op jit(solution)/shard_map/ppermute | solution.py:19
  12.8 0.3 %collective-permute-done.4 = f32[4,16,128]{2,1,0:T(8,128)S(1)} collective-permute-done((f32[4,16,128]{2,1,0:T(8,128)S(1)}, f32[4,16,128]{2,1,0:T(8,128)S(1)}, u32[]{:S(2)}, u32[]{:S(2)}) %collective-permute-start.4) | collective-permute-done | bytes 32800 | tf_op jit(solution)/shard_map/ppermute | solution.py:19
  13.1 1.4 %collective-permute-done.5 = f32[4,16,128]{2,1,0:T(8,128)S(1)} collective-permute-done((f32[4,16,128]{2,1,0:T(8,128)S(1)}, f32[4,16,128]{2,1,0:T(8,128)S(1)}, u32[]{:S(2)}, u32[]{:S(2)}) %collective-permute-start.5) | collective-permute-done | bytes 32800 | tf_op jit(solution)/shard_map/ppermute | solution.py:19
  14.6 3.8 %collective-permute-start.6 = (f32[4,4,8,128]{3,2,1,0:T(8,128)S(1)}, f32[4,4,8,128]{3,2,1,0:T(8,128)S(1)}, u32[]{:S(2)}, u32[]{:S(2)}) collective-permute-start(f32[4,4,8,128]{3,2,1,0:T(8,128)S(1)} %dynamic-slice_bitcast_fusion), channel_id=1, source_target_pairs={{0,1},{1,0},{2,3},{3,2},{4,5},{5,4},{6,7},{7,6},{8,9},{9,8},{10,11... | collective-permute-start | bytes 196616 | tf_op jit(solution)/shard_map/ppermute | solution.py:19
  18.5 0.9 %collective-permute-done.6 = f32[4,4,8,128]{3,2,1,0:T(8,128)S(1)} collective-permute-done((f32[4,4,8,128]{3,2,1,0:T(8,128)S(1)}, f32[4,4,8,128]{3,2,1,0:T(8,128)S(1)}, u32[]{:S(2)}, u32[]{:S(2)}) %collective-permute-start.6) | collective-permute-done | bytes 65568 | tf_op jit(solution)/shard_map/ppermute | solution.py:19
  19.4 0.6 %fusion.2 = f32[3,8,128]{2,1,0:T(8,128)} fusion(f32[4,3,8,128]{3,2,1,0:T(8,128)S(1)} %fusion, f32[8,128]{1,0:T(8,128)S(1)} %multiply_bitcast_fusion, f32[8,128]{1,0:T(8,128)S(1)} %get-tuple-element.25, f32[8,128]{1,0:T(8,128)S(1)} %get-tuple-element.24, f32[8,128]{1,0:T(8,128)S(1)} %get-tuple-element.23), kind=kLoop, calls=%fused_computation.15 | loop fusion | flops 21504 | bytes 77824 | tf_op jit(solution)/shard_map/add | solution.py:250
  (10 shorter events, 0.1 us)
Async XLA Ops:
  2.0 5.0 %collective-permute-start = (f32[64,128]{1,0:T(8,128)S(1)}, f32[64,128]{1,0:T(8,128)S(1)}, u32[]{:S(2)}, u32[]{:S(2)}) collective-permute-start(f32[64,128]{1,0:T(8,128)S(1)} %get-tuple-element.10), channel_id=1, source_target_pairs={{0,24},{8,16},{16,8},{24,0},{1,25},{9,17},{17,9},{25,1},{2,26},{10... | collective-permute-start | bytes 98312 | tf_op jit(solution)/shard_map/ppermute | solution.py:19
  3.4 3.7 %collective-permute-start.1 = (f32[64,128]{1,0:T(8,128)S(1)}, f32[64,128]{1,0:T(8,128)S(1)}, u32[]{:S(2)}, u32[]{:S(2)}) collective-permute-start(f32[64,128]{1,0:T(8,128)S(1)} %get-tuple-element.10), channel_id=1, source_target_pairs={{0,16},{8,24},{16,0},{24,8},{1,17},{9,25},{17,1},{25,9},{2,18},{10... | collective-permute-start | bytes 98312 | tf_op jit(solution)/shard_map/ppermute | solution.py:19
  4.3 2.8 %collective-permute-start.2 = (f32[64,128]{1,0:T(8,128)S(1)}, f32[64,128]{1,0:T(8,128)S(1)}, u32[]{:S(2)}, u32[]{:S(2)}) collective-permute-start(f32[64,128]{1,0:T(8,128)S(1)} %get-tuple-element.10), channel_id=1, source_target_pairs={{0,8},{8,0},{16,24},{24,16},{1,9},{9,1},{17,25},{25,17},{2,10},{10... | collective-permute-start | bytes 98312 | tf_op jit(solution)/shard_map/ppermute | solution.py:19
  4.8 2.4 %copy-start = (f32[3,4]{1,0:T(4,128)S(1)}, f32[3,4]{1,0:T(4,128)}, u32[]{:S(2)}) copy-start(f32[3,4]{1,0:T(4,128)} %coef_ref.1) | copy-start | bytes 148
  9.1 3.7 %collective-permute-start.3 = (f32[4,16,128]{2,1,0:T(8,128)S(1)}, f32[4,16,128]{2,1,0:T(8,128)S(1)}, u32[]{:S(2)}, u32[]{:S(2)}) collective-permute-start(f32[4,16,128]{2,1,0:T(8,128)S(1)} %get-tuple-element.20), channel_id=1, source_target_pairs={{0,6},{1,7},{2,4},{3,5},{4,2},{5,3},{6,0},{7,1},{8,14},{9,15},{10,... | collective-permute-start | bytes 98312 | tf_op jit(solution)/shard_map/ppermute | solution.py:19
  10.3 2.9 %collective-permute-start.4 = (f32[4,16,128]{2,1,0:T(8,128)S(1)}, f32[4,16,128]{2,1,0:T(8,128)S(1)}, u32[]{:S(2)}, u32[]{:S(2)}) collective-permute-start(f32[4,16,128]{2,1,0:T(8,128)S(1)} %get-tuple-element.19), channel_id=1, source_target_pairs={{0,4},{1,5},{2,6},{3,7},{4,0},{5,1},{6,2},{7,3},{8,12},{9,13},{10,... | collective-permute-start | bytes 98312 | tf_op jit(solution)/shard_map/ppermute | solution.py:19
  11.5 3.1 %collective-permute-start.5 = (f32[4,16,128]{2,1,0:T(8,128)S(1)}, f32[4,16,128]{2,1,0:T(8,128)S(1)}, u32[]{:S(2)}, u32[]{:S(2)}) collective-permute-start(f32[4,16,128]{2,1,0:T(8,128)S(1)} %get-tuple-element.18), channel_id=1, source_target_pairs={{0,2},{1,3},{2,0},{3,1},{4,6},{5,7},{6,4},{7,5},{8,10},{9,11},{10,... | collective-permute-start | bytes 98312 | tf_op jit(solution)/shard_map/ppermute | solution.py:19
  14.6 4.7 %collective-permute-start.6 = (f32[4,4,8,128]{3,2,1,0:T(8,128)S(1)}, f32[4,4,8,128]{3,2,1,0:T(8,128)S(1)}, u32[]{:S(2)}, u32[]{:S(2)}) collective-permute-start(f32[4,4,8,128]{3,2,1,0:T(8,128)S(1)} %dynamic-slice_bitcast_fusion), channel_id=1, source_target_pairs={{0,1},{1,0},{2,3},{3,2},{4,5},{5,4},{6,7},{7,6},{8,9},{9,8},{10,11... | collective-permute-start | bytes 196616 | tf_op jit(solution)/shard_map/ppermute | solution.py:19

commit v5 on v4

--- a/solution.py
+++ b/solution.py
@@ -160,31 +160,36 @@
     step_cells,
     light_scale,
     unit,
+    picks,
+    own,
     place_ref,
+    chip_ref,
     coef_ref,
     light_ref,
     still_ref,
     shade_ref,
     value_ref,
-    out_ref,
-    reach_ref,
+    *refs,
 ):
-    cells, planes, lanes = shade_ref.shape
-    blocks = planes // HEIGHT
+    outs, refs = refs[: len(picks)], refs[len(picks) :]
+    passed, (reach_ref,) = refs[:-1], refs[-1:]
+    cells, _, lanes = shade_ref.shape
     chunks = cells // step_cells
-    def block_rows(k):
-        return pl.ds(k * HEIGHT if isinstance(k, int) else pl.multiple_of(k * HEIGHT, HEIGHT), HEIGHT)
-
-    def finish(k, moments):
-        through = still_ref[0, block_rows(k)]
+
+    def block_rows(pick):
+        if own is None:
+            return pl.ds(pick * HEIGHT, HEIGHT)
+        return pl.ds(pl.multiple_of((chip_ref[0] ^ pick) * HEIGHT, HEIGHT), HEIGHT)
+
+    def finish(out_ref, at, moments):
         for c in range(3):
-            out_ref[k, c] = sum(
+            out_ref[c] = sum(
                 coef_ref[c : c + 1, i : i + 1] * unit**i * moments[i] for i in range(4)
             )
-        out_ref[k, 3] = through
-
-    def parts(k):
-        reach = reach_ref[block_rows(k)]
+        out_ref[3] = still_ref[0, at]
+
+    def parts(at):
+        reach = reach_ref[at]
         high = reach.astype(jnp.bfloat16)
         return high, (reach - high.astype(jnp.float32)).astype(jnp.bfloat16)
 
@@ -199,9 +204,8 @@
         )
         return spread[:, :lanes], spread[:, lanes:]
 
-    def use(chunk, k, spread, state):
+    def use(chunk, at, spread, state):
         m0, m1, m2, m3 = state
-        at = block_rows(k)
         for j in range(step_cells):
             cell = chunk * step_cells + j
             value = value_ref[cell, at]
@@ -218,8 +222,9 @@
 
     @pl.when(place_ref[0] == 0)
     def _():
-        for k in range(blocks):
-            finish(k, [still_ref[1 + i, block_rows(k)] for i in range(4)])
+        for pick, out_ref in zip(picks, outs):
+            at = block_rows(pick)
+            finish(out_ref, at, [still_ref[1 + i, at] for i in range(4)])
 
     @pl.when(place_ref[0] != 0)
     def _():
@@ -227,17 +232,29 @@
         row = lax.broadcasted_iota(jnp.int32, (2 * cells, 2 * lanes), 0)
         column = lax.broadcasted_iota(jnp.int32, (2 * cells, 2 * lanes), 1)
         turns = jnp.where((row % 2 == 0) == (column < lanes), 1.0, 0.0).astype(jnp.bfloat16)
-        reach = jnp.exp2(light_ref[...] * light_scale).T
-        half = reach.shape[0] // 2
-        reach_ref[...] = jnp.concatenate([reach[:half], reach[half:]], axis=1)
-        for k in range(blocks):
-            both = parts(k)
+        if own == "take":
+            reach_ref[...] = light_ref[...]
+        else:
+            reach = jnp.exp2(light_ref[...] * light_scale).T
+            half = reach.shape[0] // 2
+            reach_ref[...] = jnp.concatenate([reach[:half], reach[half:]], axis=1)
+        if own == "pass":
+            at = block_rows(0)
+            passed[0][...] = reach_ref[at]
+            for cell in range(cells):
+                passed[1][cell] = shade_ref[cell, at]
+                passed[2][cell] = value_ref[cell, at]
+        for pick, out_ref in zip(picks, outs):
+            at = block_rows(pick)
+            table_at = slice(None) if own == "take" else at
+            both = parts(table_at)
             state = (jnp.zeros((HEIGHT, lanes), jnp.float32),) * 4
             for chunk in range(chunks):
-                state = use(chunk, k, fill(chunk, both, pair, turns), state)
-            at = block_rows(k)
+                state = use(chunk, table_at, fill(chunk, both, pair, turns), state)
             m0 = state[0] + 0.3 * (1.0 - still_ref[0, at])
-            finish(k, [m0] + [state[i] + 0.3 * still_ref[1 + i, at] for i in (1, 2, 3)])
+            finish(
+                out_ref, at, [m0] + [state[i] + 0.3 * still_ref[1 + i, at] for i in (1, 2, 3)]
+            )
 
 
 def over(pieces, order):
@@ -314,21 +331,32 @@
     for mask, other in arrived:
         upstream = upstream + jnp.where(place ^ mask < place, other, 0.0)
 
-    away = pl.pallas_call(
-        functools.partial(lit_kernel, lit_cells, light_scale, 1.0 / sum(view_parts)),
-        name="lit_kernel",
-        out_shape=jax.ShapeDtypeStruct((planes // HEIGHT, 4, HEIGHT, lanes), jnp.float32),
-        in_specs=[scalars] + [whole] * 5,
-        out_specs=whole,
-        scratch_shapes=[VMEM((planes, cells), jnp.float32)],
-        compiler_params=pltpu.CompilerParams(vmem_limit_bytes=8 * 2**20),
-    )(where, color_coef, upstream, still, shade, value)
-
-    if 2 * own_rows != HEIGHT:
-        away = jnp.swapaxes(away, 0, 1).reshape(4, chips, 2 * own_rows, lanes)
-        away = jnp.swapaxes(away, 0, 1)
-    sent = [lax.dynamic_index_in_dim(away, chip ^ mask, 0, False) for mask in others]
-    own = lax.dynamic_index_in_dim(away, chip, 0, False)
+    def lit(picks, own, light, shade, value):
+        reach = jax.ShapeDtypeStruct((HEIGHT if own == "take" else planes, cells), jnp.float32)
+        rows_table = jax.ShapeDtypeStruct((cells, HEIGHT, lanes), jnp.float32)
+        passed = []
+        if own == "pass":
+            passed = [jax.ShapeDtypeStruct((HEIGHT, cells), jnp.float32), rows_table, rows_table]
+        return pl.pallas_call(
+            functools.partial(
+                lit_kernel, lit_cells, light_scale, 1.0 / sum(view_parts), picks, own
+            ),
+            name="lit_kernel",
+            out_shape=[jax.ShapeDtypeStruct((4, HEIGHT, lanes), jnp.float32)] * len(picks) + passed,
+            in_specs=[scalars] * 2 + [whole] * 5,
+            out_specs=[whole] * (len(picks) + len(passed)),
+            scratch_shapes=[VMEM(reach.shape, reach.dtype)],
+            compiler_params=pltpu.CompilerParams(vmem_limit_bytes=8 * 2**20),
+        )(where, chip.astype(jnp.int32)[None], color_coef, light, still, shade, value)
+
+    if 2 * own_rows == HEIGHT:
+        *sent, reach, shade, value = lit(tuple(others), "pass", upstream, shade, value)
+        (own,) = lit((0,), "take", reach, shade, value)
+    else:
+        every = lit(tuple(range(planes // HEIGHT)), None, upstream, shade, value)
+        every = jnp.stack(every, axis=1).reshape(4, chips, 2 * own_rows, lanes)
+        sent = [lax.dynamic_index_in_dim(every, chip ^ mask, 1, False) for mask in others]
+        own = lax.dynamic_index_in_dim(every, chip, 1, False)
     pieces = [own] + [swapped(x, "view", 2 * mask) for x, mask in zip(sent, others)]
     order = [chip] + [chip ^ mask for mask in others]
     pieces = jnp.stack(pieces).reshape(chips, 4, 2, own_rows, lanes)

time: 20.2 us -> 19.8 us (0.980)
  the two profiles are of different devices: /device:TPU:13 before, /device:TPU:0 now
where the time goes in v5:
time: 19.8 us; the launch traced here: 19.7 us
  starting transfers between devices  8.29 us (42%)
  waiting for transfers between devices  5.87 us (30%)
  Pallas kernels  4.62 us (23%)
  other arithmetic  0.68 us (3%)
    ppermute x7, starting transfers between devices, swapped(): return lax.ppermute(x, axis, [(i, i ^ mask) for i in range(devices)])  8.29 us
    ppermute x7, waiting for transfers between devices, swapped(): return lax.ppermute(x, axis, [(i, i ^ mask) for i in range(devices)])  5.87 us
    pallas_call x1, Pallas kernels, body(): pl.pallas_call(functools.partial(local_kernel, rows, step_cells, in_parts...  2.3 us
    pallas_call x1, Pallas kernels, body(): pl.pallas_call(functools.partial(totals_kernel, chunk, light_count - 1),...  2.01 us
    add x1, other arithmetic, over(): total = total + piece[:3] * ahead[None]  0.61 us
  transfers between devices with their start and end apart: 7, of which 6 were waited for; matrix products, arithmetic and copies ran while one was open for 0% of the time, Pallas kernels for 12%

profile of v5, /device:TPU:0, one launch (start us, length us, event | category | flops | bytes accessed | tf_op | source)
XLA Modules:
  0.0 19.7 jit_solution(9244514023468971493)
XLA Ops:
  0.0 2.0 %totals_kernel.1 = (f32[64,128]{1,0:T(8,128)S(1)}, bf16[128,64,128]{2,1,0:T(8,128)(2,1)S(1)}) custom-call(s32[1]{0:T(128)} %bitcast.place_ref, bf16[128,64,128]{2,1,0:T(8,128)(2,1)} %density_ref.3), custom_call_target="tpu_custom_call" | custom-call | tf_op jit(solution)/shard_map/totals_kernel/pallas_call | solution.py:290
  2.0 3.1 %collective-permute-start = (f32[64,128]{1,0:T(8,128)S(1)}, f32[64,128]{1,0:T(8,128)S(1)}, u32[]{:S(2)}, u32[]{:S(2)}) collective-permute-start(f32[64,128]{1,0:T(8,128)S(1)} %get-tuple-element.16), channel_id=1, source_target_pairs={{0,24},{8,16},{16,8},{24,0},{1,25},{9,17},{17,9},{25,1},{2,26},{10... | collective-permute-start | bytes 98312 | tf_op jit(solution)/shard_map/ppermute | solution.py:19
  5.2 1.4 %collective-permute-start.1 = (f32[64,128]{1,0:T(8,128)S(1)}, f32[64,128]{1,0:T(8,128)S(1)}, u32[]{:S(2)}, u32[]{:S(2)}) collective-permute-start(f32[64,128]{1,0:T(8,128)S(1)} %get-tuple-element.16), channel_id=1, source_target_pairs={{0,16},{8,24},{16,0},{24,8},{1,17},{9,25},{17,1},{25,9},{2,18},{10... | collective-permute-start | bytes 98312 | tf_op jit(solution)/shard_map/ppermute | solution.py:19
  6.6 0.1 collective-permute-start.2
  6.7 0.0 copy-start
  6.8 2.3 %local_kernel.1 = (f32[128,64,128]{2,1,0:T(8,128)S(1)}, f32[128,64,128]{2,1,0:T(8,128)S(1)}, f32[5,64,128]{2,1,0:T(8,128)S(1)}) custom-call(s32[1]{0:T(128)} %bitcast.place_ref, bf16[128,64,128]{2,1,0:T(8,128)(2,1)S(1)} %brick_kernel.1.brick_ref), custom_call_target="tpu_custom_call" | custom-call | flops 20971520 | bytes 8388608 | tf_op jit(solution)/shard_map/local_kernel/pallas_call | solution.py:318
  9.1 0.0 collective-permute-done
  9.1 0.9 %collective-permute-done.1 = f32[64,128]{1,0:T(8,128)S(1)} collective-permute-done((f32[64,128]{1,0:T(8,128)S(1)}, f32[64,128]{1,0:T(8,128)S(1)}, u32[]{:S(2)}, u32[]{:S(2)}) %collective-permute-start.1) | collective-permute-done | bytes 32800 | tf_op jit(solution)/shard_map/ppermute | solution.py:19
  10.0 0.5 %collective-permute-done.2 = f32[64,128]{1,0:T(8,128)S(1)} collective-permute-done((f32[64,128]{1,0:T(8,128)S(1)}, f32[64,128]{1,0:T(8,128)S(1)}, u32[]{:S(2)}, u32[]{:S(2)}) %collective-permute-start.2) | collective-permute-done | bytes 32800 | tf_op jit(solution)/shard_map/ppermute | solution.py:19
  10.5 0.0 copy-done
  10.5 0.2 lit_kernel.2
  10.7 2.5 %collective-permute-start.3 = (f32[4,16,128]{2,1,0:T(8,128)S(1)}, f32[4,16,128]{2,1,0:T(8,128)S(1)}, u32[]{:S(2)}, u32[]{:S(2)}) collective-permute-start(f32[4,16,128]{2,1,0:T(8,128)S(1)} %get-tuple-element.24), channel_id=1, source_target_pairs={{0,6},{1,7},{2,4},{3,5},{4,2},{5,3},{6,0},{7,1},{8,14},{9,15},{10,... | collective-permute-start | bytes 98312 | tf_op jit(solution)/shard_map/ppermute | solution.py:19
  13.2 0.5 %collective-permute-start.4 = (f32[4,16,128]{2,1,0:T(8,128)S(1)}, f32[4,16,128]{2,1,0:T(8,128)S(1)}, u32[]{:S(2)}, u32[]{:S(2)}) collective-permute-start(f32[4,16,128]{2,1,0:T(8,128)S(1)} %get-tuple-element.25), channel_id=1, source_target_pairs={{0,4},{1,5},{2,6},{3,7},{4,0},{5,1},{6,2},{7,3},{8,12},{9,13},{10,... | collective-permute-start | bytes 98312 | tf_op jit(solution)/shard_map/ppermute | solution.py:19
  13.7 0.5 %collective-permute-start.5 = (f32[4,16,128]{2,1,0:T(8,128)S(1)}, f32[4,16,128]{2,1,0:T(8,128)S(1)}, u32[]{:S(2)}, u32[]{:S(2)}) collective-permute-start(f32[4,16,128]{2,1,0:T(8,128)S(1)} %get-tuple-element.26), channel_id=1, source_target_pairs={{0,2},{1,3},{2,0},{3,1},{4,6},{5,7},{6,4},{7,5},{8,10},{9,11},{10,... | collective-permute-start | bytes 98312 | tf_op jit(solution)/shard_map/ppermute | solution.py:19
  14.2 0.1 lit_kernel.3
  14.4 1.2 %collective-permute-done.3 = f32[4,16,128]{2,1,0:T(8,128)S(1)} collective-permute-done((f32[4,16,128]{2,1,0:T(8,128)S(1)}, f32[4,16,128]{2,1,0:T(8,128)S(1)}, u32[]{:S(2)}, u32[]{:S(2)}) %collective-permute-start.3) | collective-permute-done | bytes 32800 | tf_op jit(solution)/shard_map/ppermute | solution.py:19
  15.6 1.5 %collective-permute-done.4 = f32[4,16,128]{2,1,0:T(8,128)S(1)} collective-permute-done((f32[4,16,128]{2,1,0:T(8,128)S(1)}, f32[4,16,128]{2,1,0:T(8,128)S(1)}, u32[]{:S(2)}, u32[]{:S(2)}) %collective-permute-start.4) | collective-permute-done | bytes 32800 | tf_op jit(solution)/shard_map/ppermute | solution.py:19
  17.1 0.5 %collective-permute-done.5 = f32[4,16,128]{2,1,0:T(8,128)S(1)} collective-permute-done((f32[4,16,128]{2,1,0:T(8,128)S(1)}, f32[4,16,128]{2,1,0:T(8,128)S(1)}, u32[]{:S(2)}, u32[]{:S(2)}) %collective-permute-start.5) | collective-permute-done | bytes 32800 | tf_op jit(solution)/shard_map/ppermute | solution.py:19
  17.6 0.1 collective-permute-start.6
  17.8 1.2 %collective-permute-done.6 = f32[4,4,8,128]{3,2,1,0:T(8,128)S(1)} collective-permute-done((f32[4,4,8,128]{3,2,1,0:T(8,128)S(1)}, f32[4,4,8,128]{3,2,1,0:T(8,128)S(1)}, u32[]{:S(2)}, u32[]{:S(2)}) %collective-permute-start.6) | collective-permute-done | bytes 65568 | tf_op jit(solution)/shard_map/ppermute | solution.py:19
  19.0 0.6 %fusion.2 = f32[3,8,128]{2,1,0:T(8,128)} fusion(f32[4,3,8,128]{3,2,1,0:T(8,128)S(1)} %fusion, f32[8,128]{1,0:T(8,128)S(1)} %multiply_bitcast_fusion, f32[8,128]{1,0:T(8,128)S(1)} %get-tuple-element.33, f32[8,128]{1,0:T(8,128)S(1)} %get-tuple-element.32, f32[8,128]{1,0:T(8,128)S(1)} %get-tuple-element.31), kind=kLoop, calls=%fused_computation.11 | loop fusion | flops 21504 | bytes 77824 | tf_op jit(solution)/shard_map/add | solution.py:267
  (9 shorter events, 0.1 us)
Async XLA Ops:
  2.0 7.0 %collective-permute-start = (f32[64,128]{1,0:T(8,128)S(1)}, f32[64,128]{1,0:T(8,128)S(1)}, u32[]{:S(2)}, u32[]{:S(2)}) collective-permute-start(f32[64,128]{1,0:T(8,128)S(1)} %get-tuple-element.16), channel_id=1, source_target_pairs={{0,24},{8,16},{16,8},{24,0},{1,25},{9,17},{17,9},{25,1},{2,26},{10... | collective-permute-start | bytes 98312 | tf_op jit(solution)/shard_map/ppermute | solution.py:19
  5.2 4.8 %collective-permute-start.1 = (f32[64,128]{1,0:T(8,128)S(1)}, f32[64,128]{1,0:T(8,128)S(1)}, u32[]{:S(2)}, u32[]{:S(2)}) collective-permute-start(f32[64,128]{1,0:T(8,128)S(1)} %get-tuple-element.16), channel_id=1, source_target_pairs={{0,16},{8,24},{16,0},{24,8},{1,17},{9,25},{17,1},{25,9},{2,18},{10... | collective-permute-start | bytes 98312 | tf_op jit(solution)/shard_map/ppermute | solution.py:19
  6.6 3.9 %collective-permute-start.2 = (f32[64,128]{1,0:T(8,128)S(1)}, f32[64,128]{1,0:T(8,128)S(1)}, u32[]{:S(2)}, u32[]{:S(2)}) collective-permute-start(f32[64,128]{1,0:T(8,128)S(1)} %get-tuple-element.16), channel_id=1, source_target_pairs={{0,8},{8,0},{16,24},{24,16},{1,9},{9,1},{17,25},{25,17},{2,10},{10... | collective-permute-start | bytes 98312 | tf_op jit(solution)/shard_map/ppermute | solution.py:19
  6.7 3.8 %copy-start = (f32[3,4]{1,0:T(4,128)S(1)}, f32[3,4]{1,0:T(4,128)}, u32[]{:S(2)}) copy-start(f32[3,4]{1,0:T(4,128)} %coef_ref.3) | copy-start | bytes 148
  10.7 4.9 %collective-permute-start.3 = (f32[4,16,128]{2,1,0:T(8,128)S(1)}, f32[4,16,128]{2,1,0:T(8,128)S(1)}, u32[]{:S(2)}, u32[]{:S(2)}) collective-permute-start(f32[4,16,128]{2,1,0:T(8,128)S(1)} %get-tuple-element.24), channel_id=1, source_target_pairs={{0,6},{1,7},{2,4},{3,5},{4,2},{5,3},{6,0},{7,1},{8,14},{9,15},{10,... | collective-permute-start | bytes 98312 | tf_op jit(solution)/shard_map/ppermute | solution.py:19
  13.2 3.9 %collective-permute-start.4 = (f32[4,16,128]{2,1,0:T(8,128)S(1)}, f32[4,16,128]{2,1,0:T(8,128)S(1)}, u32[]{:S(2)}, u32[]{:S(2)}) collective-permute-start(f32[4,16,128]{2,1,0:T(8,128)S(1)} %get-tuple-element.25), channel_id=1, source_target_pairs={{0,4},{1,5},{2,6},{3,7},{4,0},{5,1},{6,2},{7,3},{8,12},{9,13},{10,... | collective-permute-start | bytes 98312 | tf_op jit(solution)/shard_map/ppermute | solution.py:19
  13.7 3.9 %collective-permute-start.5 = (f32[4,16,128]{2,1,0:T(8,128)S(1)}, f32[4,16,128]{2,1,0:T(8,128)S(1)}, u32[]{:S(2)}, u32[]{:S(2)}) collective-permute-start(f32[4,16,128]{2,1,0:T(8,128)S(1)} %get-tuple-element.26), channel_id=1, source_target_pairs={{0,2},{1,3},{2,0},{3,1},{4,6},{5,7},{6,4},{7,5},{8,10},{9,11},{10,... | collective-permute-start | bytes 98312 | tf_op jit(solution)/shard_map/ppermute | solution.py:19
  17.6 1.3 %collective-permute-start.6 = (f32[4,4,8,128]{3,2,1,0:T(8,128)S(1)}, f32[4,4,8,128]{3,2,1,0:T(8,128)S(1)}, u32[]{:S(2)}, u32[]{:S(2)}) collective-permute-start(f32[4,4,8,128]{3,2,1,0:T(8,128)S(1)} %dynamic-slice_bitcast_fusion), channel_id=1, source_target_pairs={{0,1},{1,0},{2,3},{3,2},{4,5},{5,4},{6,7},{7,6},{8,9},{9,8},{10,11... | collective-permute-start | bytes 196616 | tf_op jit(solution)/shard_map/ppermute | solution.py:19

commit v6 on v5

--- a/solution.py
+++ b/solution.py
@@ -11,7 +11,7 @@
 
 VMEM = pltpu.VMEM
 LOG2E = math.log2(math.e)
-HEIGHT = 16
+TILE = 8
 
 
 def swapped(x, axis, mask):
@@ -161,9 +161,10 @@
     light_scale,
     unit,
     picks,
-    own,
+    handed,
+    take,
     place_ref,
-    chip_ref,
+    mine_ref,
     coef_ref,
     light_ref,
     still_ref,
@@ -175,21 +176,30 @@
     passed, (reach_ref,) = refs[:-1], refs[-1:]
     cells, _, lanes = shade_ref.shape
     chunks = cells // step_cells
-
-    def block_rows(pick):
-        if own is None:
-            return pl.ds(pick * HEIGHT, HEIGHT)
-        return pl.ds(pl.multiple_of((chip_ref[0] ^ pick) * HEIGHT, HEIGHT), HEIGHT)
-
-    def finish(out_ref, at, moments):
-        for c in range(3):
-            out_ref[c] = sum(
-                coef_ref[c : c + 1, i : i + 1] * unit**i * moments[i] for i in range(4)
-            )
-        out_ref[3] = still_ref[0, at]
-
-    def parts(at):
-        reach = reach_ref[at]
+    chip, core = mine_ref[0] // 2, mine_ref[0] % 2
+
+    def tile(place):
+        if isinstance(place, int):
+            return pl.ds(place, TILE)
+        mask, side = place
+        return pl.ds(pl.multiple_of((2 * (chip ^ mask) + (core ^ side)) * TILE, TILE), TILE)
+
+    def rows(ref, pick, *index):
+        if take and ref is not still_ref:
+            return ref[*index]
+        return jnp.concatenate([ref[*index, tile(place)] for place in pick], axis=0)
+
+    def finish(out_ref, pick, moments):
+        color = [
+            sum(coef_ref[c : c + 1, i : i + 1] * unit**i * moments[i] for i in range(4))
+            for c in range(3)
+        ]
+        for c, x in enumerate(color + [rows(still_ref, pick, 0)]):
+            for k in range(2):
+                out_ref[k, c] = x[k * TILE : (k + 1) * TILE]
+
+    def parts(pick):
+        reach = rows(reach_ref, pick)
         high = reach.astype(jnp.bfloat16)
         return high, (reach - high.astype(jnp.float32)).astype(jnp.bfloat16)
 
@@ -204,13 +214,13 @@
         )
         return spread[:, :lanes], spread[:, lanes:]
 
-    def use(chunk, at, spread, state):
+    def use(chunk, pick, spread, state):
         m0, m1, m2, m3 = state
         for j in range(step_cells):
             cell = chunk * step_cells + j
-            value = value_ref[cell, at]
-            here = slice(j // 2 * HEIGHT, (j // 2 + 1) * HEIGHT)
-            weight = shade_ref[cell, at] * spread[j % 2][here]
+            value = rows(value_ref, pick, cell)
+            here = slice(j // 2 * 2 * TILE, (j // 2 + 1) * 2 * TILE)
+            weight = rows(shade_ref, pick, cell) * spread[j % 2][here]
             m0 = m0 + weight
             weight = weight * value
             m1 = m1 + weight
@@ -223,37 +233,35 @@
     @pl.when(place_ref[0] == 0)
     def _():
         for pick, out_ref in zip(picks, outs):
-            at = block_rows(pick)
-            finish(out_ref, at, [still_ref[1 + i, at] for i in range(4)])
+            finish(out_ref, pick, [rows(still_ref, pick, 1 + i) for i in range(4)])
 
     @pl.when(place_ref[0] != 0)
     def _():
-        pair = lax.broadcasted_iota(jnp.int32, (HEIGHT, cells), 1) // 2
+        pair = lax.broadcasted_iota(jnp.int32, (2 * TILE, cells), 1) // 2
         row = lax.broadcasted_iota(jnp.int32, (2 * cells, 2 * lanes), 0)
         column = lax.broadcasted_iota(jnp.int32, (2 * cells, 2 * lanes), 1)
         turns = jnp.where((row % 2 == 0) == (column < lanes), 1.0, 0.0).astype(jnp.bfloat16)
-        if own == "take":
+        if take:
             reach_ref[...] = light_ref[...]
         else:
             reach = jnp.exp2(light_ref[...] * light_scale).T
             half = reach.shape[0] // 2
             reach_ref[...] = jnp.concatenate([reach[:half], reach[half:]], axis=1)
-        if own == "pass":
-            at = block_rows(0)
-            passed[0][...] = reach_ref[at]
+        if handed is not None:
+            passed[0][...] = rows(reach_ref, handed)
             for cell in range(cells):
-                passed[1][cell] = shade_ref[cell, at]
-                passed[2][cell] = value_ref[cell, at]
+                passed[1][cell] = rows(shade_ref, handed, cell)
+                passed[2][cell] = rows(value_ref, handed, cell)
         for pick, out_ref in zip(picks, outs):
-            at = block_rows(pick)
-            table_at = slice(None) if own == "take" else at
-            both = parts(table_at)
-            state = (jnp.zeros((HEIGHT, lanes), jnp.float32),) * 4
+            both = parts(pick)
+            state = (jnp.zeros((2 * TILE, lanes), jnp.float32),) * 4
             for chunk in range(chunks):
-                state = use(chunk, table_at, fill(chunk, both, pair, turns), state)
-            m0 = state[0] + 0.3 * (1.0 - still_ref[0, at])
+                state = use(chunk, pick, fill(chunk, both, pair, turns), state)
+            m0 = state[0] + 0.3 * (1.0 - rows(still_ref, pick, 0))
             finish(
-                out_ref, at, [m0] + [state[i] + 0.3 * still_ref[1 + i, at] for i in (1, 2, 3)]
+                out_ref,
+                pick,
+                [m0] + [state[i] + 0.3 * rows(still_ref, pick, 1 + i) for i in (1, 2, 3)],
             )
 
 
@@ -313,7 +321,6 @@
     mine = lax.axis_index("view")
     core, chip = mine % 2, mine // 2
     chips = view_count // 2
-    others = list(range(chips - 1, 0, -1))
     table = jax.ShapeDtypeStruct(density.shape, jnp.float32)
     shade, value, still = pl.pallas_call(
         functools.partial(local_kernel, rows, step_cells, in_parts(light_scale), view_parts),
@@ -331,42 +338,54 @@
     for mask, other in arrived:
         upstream = upstream + jnp.where(place ^ mask < place, other, 0.0)
 
-    def lit(picks, own, light, shade, value):
-        reach = jax.ShapeDtypeStruct((HEIGHT if own == "take" else planes, cells), jnp.float32)
-        rows_table = jax.ShapeDtypeStruct((cells, HEIGHT, lanes), jnp.float32)
+    def lit(picks, light, shade, value, handed=None, take=False):
+        reach = jax.ShapeDtypeStruct((2 * TILE if take else planes, cells), jnp.float32)
+        table = jax.ShapeDtypeStruct((cells, 2 * TILE, lanes), jnp.float32)
         passed = []
-        if own == "pass":
-            passed = [jax.ShapeDtypeStruct((HEIGHT, cells), jnp.float32), rows_table, rows_table]
+        if handed is not None:
+            passed = [jax.ShapeDtypeStruct((2 * TILE, cells), jnp.float32), table, table]
         return pl.pallas_call(
             functools.partial(
-                lit_kernel, lit_cells, light_scale, 1.0 / sum(view_parts), picks, own
+                lit_kernel, lit_cells, light_scale, 1.0 / sum(view_parts), picks, handed, take
             ),
             name="lit_kernel",
-            out_shape=[jax.ShapeDtypeStruct((4, HEIGHT, lanes), jnp.float32)] * len(picks) + passed,
+            out_shape=[jax.ShapeDtypeStruct((2, 4, TILE, lanes), jnp.float32)] * len(picks) + passed,
             in_specs=[scalars] * 2 + [whole] * 5,
             out_specs=[whole] * (len(picks) + len(passed)),
             scratch_shapes=[VMEM(reach.shape, reach.dtype)],
             compiler_params=pltpu.CompilerParams(vmem_limit_bytes=8 * 2**20),
-        )(where, chip.astype(jnp.int32)[None], color_coef, light, still, shade, value)
-
-    if 2 * own_rows == HEIGHT:
-        *sent, reach, shade, value = lit(tuple(others), "pass", upstream, shade, value)
-        (own,) = lit((0,), "take", reach, shade, value)
+        )(where, mine.astype(jnp.int32)[None], color_coef, light, still, shade, value)
+
+    order = list(range(chips - 1, -1, -1))
+    if own_rows == TILE and chips % 2 == 0:
+        pairs = list(zip(order[::2], order[1::2]))
+        give_picks = tuple(tuple((mask, 1) for mask in two) for two in pairs)
+        keep_picks = tuple(tuple((mask, 0) for mask in two) for two in pairs)
+        split = len(pairs)
+        *first, reach, shade, value = lit(
+            give_picks + keep_picks[:-1], upstream, shade, value, handed=keep_picks[-1]
+        )
+        give = jnp.concatenate(first[:split], axis=0)
+        took = swapped(give, "view", 1)
+        keep = jnp.concatenate(
+            [*first[split:], *lit(keep_picks[-1:], reach, shade, value, take=True)], axis=0
+        )
     else:
-        every = lit(tuple(range(planes // HEIGHT)), None, upstream, shade, value)
-        every = jnp.stack(every, axis=1).reshape(4, chips, 2 * own_rows, lanes)
-        sent = [lax.dynamic_index_in_dim(every, chip ^ mask, 1, False) for mask in others]
-        own = lax.dynamic_index_in_dim(every, chip, 1, False)
-    pieces = [own] + [swapped(x, "view", 2 * mask) for x, mask in zip(sent, others)]
-    order = [chip] + [chip ^ mask for mask in others]
-    pieces = jnp.stack(pieces).reshape(chips, 4, 2, own_rows, lanes)
-    keep = lax.dynamic_index_in_dim(pieces, core, 2, False)
-    took = swapped(lax.dynamic_index_in_dim(pieces, 1 - core, 2, False), "view", 1)
+        picks = tuple((z, z + TILE) for z in range(0, planes, 2 * TILE))
+        every = jnp.concatenate(lit(picks, upstream, shade, value), axis=0)
+        every = jnp.swapaxes(every, 0, 1).reshape(4, chips, 2, own_rows, lanes)
+        every = jnp.stack(
+            [lax.dynamic_index_in_dim(every, chip ^ mask, 1, False) for mask in order]
+        )
+        give = lax.dynamic_index_in_dim(every, 1 - core, 2, False)
+        keep = lax.dynamic_index_in_dim(every, core, 2, False)
+        took = swapped(give, "view", 1)
     near = jnp.where(core == 0, keep, took)
     far = jnp.where(core == 0, took, keep)
     color = near[:, :3] + near[:, 3:] * far[:, :3]
     both = jnp.concatenate([color, near[:, 3:] * far[:, 3:]], axis=1)
-    return over([both[k] for k in range(chips)], order)
+    pieces = [swapped(both[k], "view", 2 * mask) for k, mask in enumerate(order[:-1])] + [both[-1]]
+    return over(pieces, [chip ^ mask for mask in order])
 
 
 def solution(mesh):

time: 19.8 us -> 19.6 us (0.990)
  transfers between devices with their start and end apart: 7 -> 7, of which waited for: 6 -> 6; matrix products, arithmetic and copies ran while one was open for 0% -> 0% of each run, Pallas kernels for 12% -> 13%
where the time goes in v6:
time: 19.6 us; the launch traced here: 19.5 us
  starting transfers between devices  8.29 us (42%)
  waiting for transfers between devices  5.71 us (29%)
  Pallas kernels  4.63 us (24%)
  other arithmetic  0.68 us (3%)
    ppermute x7, starting transfers between devices, swapped(): return lax.ppermute(x, axis, [(i, i ^ mask) for i in range(devices)])  8.29 us
    ppermute x7, waiting for transfers between devices, swapped(): return lax.ppermute(x, axis, [(i, i ^ mask) for i in range(devices)])  5.71 us
    pallas_call x1, Pallas kernels, body(): pl.pallas_call(functools.partial(local_kernel, rows, step_cells, in_parts...  2.29 us
    pallas_call x1, Pallas kernels, body(): pl.pallas_call(functools.partial(totals_kernel, chunk, light_count - 1),...  2.01 us
    add x1, other arithmetic, over(): total = total + piece[:3] * ahead[None]  0.61 us
  transfers between devices with their start and end apart: 7, of which 6 were waited for; matrix products, arithmetic and copies ran while one was open for 0% of the time, Pallas kernels for 13%

profile of v6, /device:TPU:0, one launch (start us, length us, event | category | flops | bytes accessed | tf_op | source)
XLA Modules:
  0.0 19.5 jit_solution(7802310264681596232)
XLA Ops:
  0.0 2.0 %totals_kernel.1 = (f32[64,128]{1,0:T(8,128)S(1)}, bf16[128,64,128]{2,1,0:T(8,128)(2,1)S(1)}) custom-call(s32[1]{0:T(128)} %bitcast.place_ref, bf16[128,64,128]{2,1,0:T(8,128)(2,1)} %density_ref.3), custom_call_target="tpu_custom_call" | custom-call | tf_op jit(solution)/shard_map/totals_kernel/pallas_call | solution.py:298
  2.0 3.1 %collective-permute-start = (f32[64,128]{1,0:T(8,128)S(1)}, f32[64,128]{1,0:T(8,128)S(1)}, u32[]{:S(2)}, u32[]{:S(2)}) collective-permute-start(f32[64,128]{1,0:T(8,128)S(1)} %get-tuple-element.16), channel_id=1, source_target_pairs={{0,24},{8,16},{16,8},{24,0},{1,25},{9,17},{17,9},{25,1},{2,26},{10... | collective-permute-start | bytes 98312 | tf_op jit(solution)/shard_map/ppermute | solution.py:19
  5.2 1.4 %collective-permute-start.1 = (f32[64,128]{1,0:T(8,128)S(1)}, f32[64,128]{1,0:T(8,128)S(1)}, u32[]{:S(2)}, u32[]{:S(2)}) collective-permute-start(f32[64,128]{1,0:T(8,128)S(1)} %get-tuple-element.16), channel_id=1, source_target_pairs={{0,16},{8,24},{16,0},{24,8},{1,17},{9,25},{17,1},{25,9},{2,18},{10... | collective-permute-start | bytes 98312 | tf_op jit(solution)/shard_map/ppermute | solution.py:19
  6.6 0.1 collective-permute-start.2
  6.7 0.0 copy-start
  6.7 2.3 %local_kernel.1 = (f32[128,64,128]{2,1,0:T(8,128)S(1)}, f32[128,64,128]{2,1,0:T(8,128)S(1)}, f32[5,64,128]{2,1,0:T(8,128)S(1)}) custom-call(s32[1]{0:T(128)} %bitcast.place_ref, bf16[128,64,128]{2,1,0:T(8,128)(2,1)S(1)} %brick_kernel.1.brick_ref), custom_call_target="tpu_custom_call" | custom-call | flops 20971520 | bytes 8388608 | tf_op jit(solution)/shard_map/local_kernel/pallas_call | solution.py:325
  9.0 0.0 collective-permute-done
  9.1 0.9 %collective-permute-done.1 = f32[64,128]{1,0:T(8,128)S(1)} collective-permute-done((f32[64,128]{1,0:T(8,128)S(1)}, f32[64,128]{1,0:T(8,128)S(1)}, u32[]{:S(2)}, u32[]{:S(2)}) %collective-permute-start.1) | collective-permute-done | bytes 32800 | tf_op jit(solution)/shard_map/ppermute | solution.py:19
  10.0 0.5 %collective-permute-done.2 = f32[64,128]{1,0:T(8,128)S(1)} collective-permute-done((f32[64,128]{1,0:T(8,128)S(1)}, f32[64,128]{1,0:T(8,128)S(1)}, u32[]{:S(2)}, u32[]{:S(2)}) %collective-permute-start.2) | collective-permute-done | bytes 32800 | tf_op jit(solution)/shard_map/ppermute | solution.py:19
  10.5 0.0 copy-done
  10.5 0.2 lit_kernel.2
  10.7 0.1 collective-permute-start.3
  10.8 0.1 lit_kernel.3
  10.9 1.1 %collective-permute-done.3 = f32[4,4,8,128]{3,2,1,0:T(8,128)S(1)} collective-permute-done((f32[4,4,8,128]{3,2,1,0:T(8,128)S(1)}, f32[4,4,8,128]{3,2,1,0:T(8,128)S(1)}, u32[]{:S(2)}, u32[]{:S(2)}) %collective-permute-start.3) | collective-permute-done | bytes 65568 | tf_op jit(solution)/shard_map/ppermute | solution.py:19
  12.1 2.5 %collective-permute-start.4 = (f32[4,8,128]{2,1,0:T(8,128)S(1)}, f32[4,8,128]{2,1,0:T(8,128)S(1)}, u32[]{:S(2)}, u32[]{:S(2)}) collective-permute-start(f32[4,8,128]{2,1,0:T(8,128)S(1)} %get-tuple-element.29), channel_id=1, source_target_pairs={{0,6},{1,7},{2,4},{3,5},{4,2},{5,3},{6,0},{7,1},{8,14},{9,15},{10,... | collective-permute-start | bytes 49160 | tf_op jit(solution)/shard_map/ppermute | solution.py:19
  14.6 0.5 %collective-permute-start.5 = (f32[4,8,128]{2,1,0:T(8,128)S(1)}, f32[4,8,128]{2,1,0:T(8,128)S(1)}, u32[]{:S(2)}, u32[]{:S(2)}) collective-permute-start(f32[4,8,128]{2,1,0:T(8,128)S(1)} %get-tuple-element.30), channel_id=1, source_target_pairs={{0,4},{1,5},{2,6},{3,7},{4,0},{5,1},{6,2},{7,3},{8,12},{9,13},{10,... | collective-permute-start | bytes 49160 | tf_op jit(solution)/shard_map/ppermute | solution.py:19
  15.1 0.5 %collective-permute-start.6 = (f32[4,8,128]{2,1,0:T(8,128)S(1)}, f32[4,8,128]{2,1,0:T(8,128)S(1)}, u32[]{:S(2)}, u32[]{:S(2)}) collective-permute-start(f32[4,8,128]{2,1,0:T(8,128)S(1)} %get-tuple-element.31), channel_id=1, source_target_pairs={{0,2},{1,3},{2,0},{3,1},{4,6},{5,7},{6,4},{7,5},{8,10},{9,11},{10,... | collective-permute-start | bytes 49160 | tf_op jit(solution)/shard_map/ppermute | solution.py:19
  15.6 1.1 %collective-permute-done.4 = f32[4,8,128]{2,1,0:T(8,128)S(1)} collective-permute-done((f32[4,8,128]{2,1,0:T(8,128)S(1)}, f32[4,8,128]{2,1,0:T(8,128)S(1)}, u32[]{:S(2)}, u32[]{:S(2)}) %collective-permute-start.4) | collective-permute-done | bytes 16416 | tf_op jit(solution)/shard_map/ppermute | solution.py:19
  16.8 1.5 %collective-permute-done.5 = f32[4,8,128]{2,1,0:T(8,128)S(1)} collective-permute-done((f32[4,8,128]{2,1,0:T(8,128)S(1)}, f32[4,8,128]{2,1,0:T(8,128)S(1)}, u32[]{:S(2)}, u32[]{:S(2)}) %collective-permute-start.5) | collective-permute-done | bytes 16416 | tf_op jit(solution)/shard_map/ppermute | solution.py:19
  18.3 0.5 %collective-permute-done.6 = f32[4,8,128]{2,1,0:T(8,128)S(1)} collective-permute-done((f32[4,8,128]{2,1,0:T(8,128)S(1)}, f32[4,8,128]{2,1,0:T(8,128)S(1)}, u32[]{:S(2)}, u32[]{:S(2)}) %collective-permute-start.6) | collective-permute-done | bytes 16416 | tf_op jit(solution)/shard_map/ppermute | solution.py:19
  18.8 0.6 %fusion.5 = f32[3,8,128]{2,1,0:T(8,128)} fusion(f32[4,3,8,128]{3,2,1,0:T(8,128)S(1)} %fusion.2, f32[4,8,128]{2,1,0:T(8,128)S(1)} %collective-permute-done.6, f32[4,8,128]{2,1,0:T(8,128)S(1)} %collective-permute-done.5, f32[4,8,128]{2,1,0:T(8,128)S(1)} %collective-permute-done.4, f32[8,128]{1,0:T(8,128)S(1)} %get-tuple-element.35, f32[8,128]{1,0:T(8,128)S(1)} %fusion.8, ...), kind=kLoop, calls=%fused_computation.15 | loop fusion | flops 21504 | bytes 77824 | tf_op jit(solution)/shard_map/add | solution.py:275
  (9 shorter events, 0.1 us)
Async XLA Ops:
  2.0 7.0 %collective-permute-start = (f32[64,128]{1,0:T(8,128)S(1)}, f32[64,128]{1,0:T(8,128)S(1)}, u32[]{:S(2)}, u32[]{:S(2)}) collective-permute-start(f32[64,128]{1,0:T(8,128)S(1)} %get-tuple-element.16), channel_id=1, source_target_pairs={{0,24},{8,16},{16,8},{24,0},{1,25},{9,17},{17,9},{25,1},{2,26},{10... | collective-permute-start | bytes 98312 | tf_op jit(solution)/shard_map/ppermute | solution.py:19
  5.2 4.8 %collective-permute-start.1 = (f32[64,128]{1,0:T(8,128)S(1)}, f32[64,128]{1,0:T(8,128)S(1)}, u32[]{:S(2)}, u32[]{:S(2)}) collective-permute-start(f32[64,128]{1,0:T(8,128)S(1)} %get-tuple-element.16), channel_id=1, source_target_pairs={{0,16},{8,24},{16,0},{24,8},{1,17},{9,25},{17,1},{25,9},{2,18},{10... | collective-permute-start | bytes 98312 | tf_op jit(solution)/shard_map/ppermute | solution.py:19
  6.6 3.9 %collective-permute-start.2 = (f32[64,128]{1,0:T(8,128)S(1)}, f32[64,128]{1,0:T(8,128)S(1)}, u32[]{:S(2)}, u32[]{:S(2)}) collective-permute-start(f32[64,128]{1,0:T(8,128)S(1)} %get-tuple-element.16), channel_id=1, source_target_pairs={{0,8},{8,0},{16,24},{24,16},{1,9},{9,1},{17,25},{25,17},{2,10},{10... | collective-permute-start | bytes 98312 | tf_op jit(solution)/shard_map/ppermute | solution.py:19
  6.7 3.8 %copy-start = (f32[3,4]{1,0:T(4,128)S(1)}, f32[3,4]{1,0:T(4,128)}, u32[]{:S(2)}) copy-start(f32[3,4]{1,0:T(4,128)} %coef_ref.3) | copy-start | bytes 148
  10.7 1.3 %collective-permute-start.3 = (f32[4,4,8,128]{3,2,1,0:T(8,128)S(1)}, f32[4,4,8,128]{3,2,1,0:T(8,128)S(1)}, u32[]{:S(2)}, u32[]{:S(2)}) collective-permute-start(f32[4,4,8,128]{3,2,1,0:T(8,128)S(1)} %pad_maximum_fusion.1), channel_id=1, source_target_pairs={{0,1},{1,0},{2,3},{3,2},{4,5},{5,4},{6,7},{7,6},{8,9},{9,8},{10,11... | collective-permute-start | bytes 196616 | tf_op jit(solution)/shard_map/ppermute | solution.py:19
  12.1 4.7 %collective-permute-start.4 = (f32[4,8,128]{2,1,0:T(8,128)S(1)}, f32[4,8,128]{2,1,0:T(8,128)S(1)}, u32[]{:S(2)}, u32[]{:S(2)}) collective-permute-start(f32[4,8,128]{2,1,0:T(8,128)S(1)} %get-tuple-element.29), channel_id=1, source_target_pairs={{0,6},{1,7},{2,4},{3,5},{4,2},{5,3},{6,0},{7,1},{8,14},{9,15},{10,... | collective-permute-start | bytes 49160 | tf_op jit(solution)/shard_map/ppermute | solution.py:19
  14.6 3.7 %collective-permute-start.5 = (f32[4,8,128]{2,1,0:T(8,128)S(1)}, f32[4,8,128]{2,1,0:T(8,128)S(1)}, u32[]{:S(2)}, u32[]{:S(2)}) collective-permute-start(f32[4,8,128]{2,1,0:T(8,128)S(1)} %get-tuple-element.30), channel_id=1, source_target_pairs={{0,4},{1,5},{2,6},{3,7},{4,0},{5,1},{6,2},{7,3},{8,12},{9,13},{10,... | collective-permute-start | bytes 49160 | tf_op jit(solution)/shard_map/ppermute | solution.py:19
  15.1 3.7 %collective-permute-start.6 = (f32[4,8,128]{2,1,0:T(8,128)S(1)}, f32[4,8,128]{2,1,0:T(8,128)S(1)}, u32[]{:S(2)}, u32[]{:S(2)}) collective-permute-start(f32[4,8,128]{2,1,0:T(8,128)S(1)} %get-tuple-element.31), channel_id=1, source_target_pairs={{0,2},{1,3},{2,0},{3,1},{4,6},{5,7},{6,4},{7,5},{8,10},{9,11},{10,... | collective-permute-start | bytes 49160 | tf_op jit(solution)/shard_map/ppermute | solution.py:19

commit v7 on v6

--- a/solution.py
+++ b/solution.py
@@ -161,6 +161,7 @@
     light_scale,
     unit,
     picks,
+    joined,
     handed,
     take,
     place_ref,
@@ -172,7 +173,9 @@
     value_ref,
     *refs,
 ):
-    outs, refs = refs[: len(picks)], refs[len(picks) :]
+    outs = [refs[0].at[pl.ds(2 * k, 2)] for k in range(joined)]
+    count = len(picks) - joined
+    outs, refs = outs + list(refs[1 : 1 + count]), refs[1 + count :]
     passed, (reach_ref,) = refs[:-1], refs[-1:]
     cells, _, lanes = shade_ref.shape
     chunks = cells // step_cells
@@ -286,7 +289,7 @@
     chunk = 32
     step_cells = 32
     rows = 16
-    lit_cells = 32
+    lit_cells = 16
     whole = pl.BlockSpec(memory_space=VMEM)
     scalars = pl.BlockSpec(memory_space=pltpu.SMEM)
 
@@ -338,7 +341,7 @@
     for mask, other in arrived:
         upstream = upstream + jnp.where(place ^ mask < place, other, 0.0)
 
-    def lit(picks, light, shade, value, handed=None, take=False):
+    def lit(picks, light, shade, value, joined=1, handed=None, take=False):
         reach = jax.ShapeDtypeStruct((2 * TILE if take else planes, cells), jnp.float32)
         table = jax.ShapeDtypeStruct((cells, 2 * TILE, lanes), jnp.float32)
         passed = []
@@ -346,12 +349,23 @@
             passed = [jax.ShapeDtypeStruct((2 * TILE, cells), jnp.float32), table, table]
         return pl.pallas_call(
             functools.partial(
-                lit_kernel, lit_cells, light_scale, 1.0 / sum(view_parts), picks, handed, take
+                lit_kernel,
+                lit_cells,
+                light_scale,
+                1.0 / sum(view_parts),
+                picks,
+                joined,
+                handed,
+                take,
             ),
             name="lit_kernel",
-            out_shape=[jax.ShapeDtypeStruct((2, 4, TILE, lanes), jnp.float32)] * len(picks) + passed,
+            out_shape=[
+                jax.ShapeDtypeStruct((2 * k, 4, TILE, lanes), jnp.float32)
+                for k in [joined] + [1] * (len(picks) - joined)
+            ]
+            + passed,
             in_specs=[scalars] * 2 + [whole] * 5,
-            out_specs=[whole] * (len(picks) + len(passed)),
+            out_specs=[whole] * (1 + len(picks) - joined + len(passed)),
             scratch_shapes=[VMEM(reach.shape, reach.dtype)],
             compiler_params=pltpu.CompilerParams(vmem_limit_bytes=8 * 2**20),
         )(where, mine.astype(jnp.int32)[None], color_coef, light, still, shade, value)
@@ -362,13 +376,17 @@
         give_picks = tuple(tuple((mask, 1) for mask in two) for two in pairs)
         keep_picks = tuple(tuple((mask, 0) for mask in two) for two in pairs)
         split = len(pairs)
-        *first, reach, shade, value = lit(
-            give_picks + keep_picks[:-1], upstream, shade, value, handed=keep_picks[-1]
+        give, *first, reach, shade, value = lit(
+            give_picks + keep_picks[:-1],
+            upstream,
+            shade,
+            value,
+            joined=split,
+            handed=keep_picks[-1],
         )
-        give = jnp.concatenate(first[:split], axis=0)
         took = swapped(give, "view", 1)
         keep = jnp.concatenate(
-            [*first[split:], *lit(keep_picks[-1:], reach, shade, value, take=True)], axis=0
+            [*first, *lit(keep_picks[-1:], reach, shade, value, take=True)], axis=0
         )
     else:
         picks = tuple((z, z + TILE) for z in range(0, planes, 2 * TILE))

time: 19.6 us -> 19.6 us (level)
  no operation moved by 1% of the time
where the time goes in v7:
time: 19.6 us; the launch traced here: 19.4 us
  starting transfers between devices  8.29 us (42%)
  waiting for transfers between devices  5.71 us (29%)
  Pallas kernels  4.63 us (24%)
  other arithmetic  0.67 us (3%)
    ppermute x7, starting transfers between devices, swapped(): return lax.ppermute(x, axis, [(i, i ^ mask) for i in range(devices)])  8.29 us
    ppermute x7, waiting for transfers between devices, swapped(): return lax.ppermute(x, axis, [(i, i ^ mask) for i in range(devices)])  5.71 us
    pallas_call x1, Pallas kernels, body(): pl.pallas_call(functools.partial(local_kernel, rows, step_cells, in_parts...  2.29 us
    pallas_call x1, Pallas kernels, body(): pl.pallas_call(functools.partial(totals_kernel, chunk, light_count - 1),...  2.01 us
    add x1, other arithmetic, over(): total = total + piece[:3] * ahead[None]  0.61 us
  transfers between devices with their start and end apart: 7, of which 6 were waited for; matrix products, arithmetic and copies ran while one was open for 0% of the time, Pallas kernels for 13%

profile of v7, /device:TPU:0, one launch (start us, length us, event | category | flops | bytes accessed | tf_op | source)
XLA Modules:
  0.0 19.4 jit_solution(3404867534894179346)
XLA Ops:
  0.0 2.0 %totals_kernel.1 = (f32[64,128]{1,0:T(8,128)S(1)}, bf16[128,64,128]{2,1,0:T(8,128)(2,1)S(1)}) custom-call(s32[1]{0:T(128)} %bitcast.place_ref, bf16[128,64,128]{2,1,0:T(8,128)(2,1)} %density_ref.3), custom_call_target="tpu_custom_call" | custom-call | tf_op jit(solution)/shard_map/totals_kernel/pallas_call | solution.py:301
  2.0 3.1 %collective-permute-start = (f32[64,128]{1,0:T(8,128)S(1)}, f32[64,128]{1,0:T(8,128)S(1)}, u32[]{:S(2)}, u32[]{:S(2)}) collective-permute-start(f32[64,128]{1,0:T(8,128)S(1)} %get-tuple-element.15), channel_id=1, source_target_pairs={{0,24},{8,16},{16,8},{24,0},{1,25},{9,17},{17,9},{25,1},{2,26},{10... | collective-permute-start | bytes 98312 | tf_op jit(solution)/shard_map/ppermute | solution.py:19
  5.2 1.4 %collective-permute-start.1 = (f32[64,128]{1,0:T(8,128)S(1)}, f32[64,128]{1,0:T(8,128)S(1)}, u32[]{:S(2)}, u32[]{:S(2)}) collective-permute-start(f32[64,128]{1,0:T(8,128)S(1)} %get-tuple-element.15), channel_id=1, source_target_pairs={{0,16},{8,24},{16,0},{24,8},{1,17},{9,25},{17,1},{25,9},{2,18},{10... | collective-permute-start | bytes 98312 | tf_op jit(solution)/shard_map/ppermute | solution.py:19
  6.6 0.1 collective-permute-start.2
  6.7 0.0 copy-start
  6.7 2.3 %local_kernel.1 = (f32[128,64,128]{2,1,0:T(8,128)S(1)}, f32[128,64,128]{2,1,0:T(8,128)S(1)}, f32[5,64,128]{2,1,0:T(8,128)S(1)}) custom-call(s32[1]{0:T(128)} %bitcast.place_ref, bf16[128,64,128]{2,1,0:T(8,128)(2,1)S(1)} %brick_kernel.1.brick_ref), custom_call_target="tpu_custom_call" | custom-call | flops 20971520 | bytes 8388608 | tf_op jit(solution)/shard_map/local_kernel/pallas_call | solution.py:328
  9.0 0.0 collective-permute-done
  9.1 0.9 %collective-permute-done.1 = f32[64,128]{1,0:T(8,128)S(1)} collective-permute-done((f32[64,128]{1,0:T(8,128)S(1)}, f32[64,128]{1,0:T(8,128)S(1)}, u32[]{:S(2)}, u32[]{:S(2)}) %collective-permute-start.1) | collective-permute-done | bytes 32800 | tf_op jit(solution)/shard_map/ppermute | solution.py:19
  10.0 0.5 %collective-permute-done.2 = f32[64,128]{1,0:T(8,128)S(1)} collective-permute-done((f32[64,128]{1,0:T(8,128)S(1)}, f32[64,128]{1,0:T(8,128)S(1)}, u32[]{:S(2)}, u32[]{:S(2)}) %collective-permute-start.2) | collective-permute-done | bytes 32800 | tf_op jit(solution)/shard_map/ppermute | solution.py:19
  10.5 0.0 copy-done
  10.5 0.2 lit_kernel.2
  10.7 0.1 collective-permute-start.3
  10.8 0.1 lit_kernel.3
  10.9 1.1 %collective-permute-done.3 = f32[4,4,8,128]{3,2,1,0:T(8,128)S(1)} collective-permute-done((f32[4,4,8,128]{3,2,1,0:T(8,128)S(1)}, f32[4,4,8,128]{3,2,1,0:T(8,128)S(1)}, u32[]{:S(2)}, u32[]{:S(2)}) %collective-permute-start.3) | collective-permute-done | bytes 65568 | tf_op jit(solution)/shard_map/ppermute | solution.py:19
  12.1 2.5 %collective-permute-start.4 = (f32[4,8,128]{2,1,0:T(8,128)S(1)}, f32[4,8,128]{2,1,0:T(8,128)S(1)}, u32[]{:S(2)}, u32[]{:S(2)}) collective-permute-start(f32[4,8,128]{2,1,0:T(8,128)S(1)} %get-tuple-element.27), channel_id=1, source_target_pairs={{0,6},{1,7},{2,4},{3,5},{4,2},{5,3},{6,0},{7,1},{8,14},{9,15},{10,... | collective-permute-start | bytes 49160 | tf_op jit(solution)/shard_map/ppermute | solution.py:19
  14.6 0.5 %collective-permute-start.5 = (f32[4,8,128]{2,1,0:T(8,128)S(1)}, f32[4,8,128]{2,1,0:T(8,128)S(1)}, u32[]{:S(2)}, u32[]{:S(2)}) collective-permute-start(f32[4,8,128]{2,1,0:T(8,128)S(1)} %get-tuple-element.28), channel_id=1, source_target_pairs={{0,4},{1,5},{2,6},{3,7},{4,0},{5,1},{6,2},{7,3},{8,12},{9,13},{10,... | collective-permute-start | bytes 49160 | tf_op jit(solution)/shard_map/ppermute | solution.py:19
  15.1 0.5 %collective-permute-start.6 = (f32[4,8,128]{2,1,0:T(8,128)S(1)}, f32[4,8,128]{2,1,0:T(8,128)S(1)}, u32[]{:S(2)}, u32[]{:S(2)}) collective-permute-start(f32[4,8,128]{2,1,0:T(8,128)S(1)} %get-tuple-element.29), channel_id=1, source_target_pairs={{0,2},{1,3},{2,0},{3,1},{4,6},{5,7},{6,4},{7,5},{8,10},{9,11},{10,... | collective-permute-start | bytes 49160 | tf_op jit(solution)/shard_map/ppermute | solution.py:19
  15.6 1.1 %collective-permute-done.4 = f32[4,8,128]{2,1,0:T(8,128)S(1)} collective-permute-done((f32[4,8,128]{2,1,0:T(8,128)S(1)}, f32[4,8,128]{2,1,0:T(8,128)S(1)}, u32[]{:S(2)}, u32[]{:S(2)}) %collective-permute-start.4) | collective-permute-done | bytes 16416 | tf_op jit(solution)/shard_map/ppermute | solution.py:19
  16.8 1.5 %collective-permute-done.5 = f32[4,8,128]{2,1,0:T(8,128)S(1)} collective-permute-done((f32[4,8,128]{2,1,0:T(8,128)S(1)}, f32[4,8,128]{2,1,0:T(8,128)S(1)}, u32[]{:S(2)}, u32[]{:S(2)}) %collective-permute-start.5) | collective-permute-done | bytes 16416 | tf_op jit(solution)/shard_map/ppermute | solution.py:19
  18.3 0.5 %collective-permute-done.6 = f32[4,8,128]{2,1,0:T(8,128)S(1)} collective-permute-done((f32[4,8,128]{2,1,0:T(8,128)S(1)}, f32[4,8,128]{2,1,0:T(8,128)S(1)}, u32[]{:S(2)}, u32[]{:S(2)}) %collective-permute-start.6) | collective-permute-done | bytes 16416 | tf_op jit(solution)/shard_map/ppermute | solution.py:19
  18.8 0.6 %fusion.5 = f32[3,8,128]{2,1,0:T(8,128)} fusion(f32[4,3,8,128]{3,2,1,0:T(8,128)S(1)} %fusion.2, f32[4,8,128]{2,1,0:T(8,128)S(1)} %collective-permute-done.6, f32[4,8,128]{2,1,0:T(8,128)S(1)} %collective-permute-done.5, f32[4,8,128]{2,1,0:T(8,128)S(1)} %collective-permute-done.4, f32[8,128]{1,0:T(8,128)S(1)} %get-tuple-element.33, f32[8,128]{1,0:T(8,128)S(1)} %fusion.8, ...), kind=kLoop, calls=%fused_computation.14 | loop fusion | flops 21504 | bytes 77824 | tf_op jit(solution)/shard_map/add | solution.py:278
  (8 shorter events, 0.1 us)
Async XLA Ops:
  2.0 7.0 %collective-permute-start = (f32[64,128]{1,0:T(8,128)S(1)}, f32[64,128]{1,0:T(8,128)S(1)}, u32[]{:S(2)}, u32[]{:S(2)}) collective-permute-start(f32[64,128]{1,0:T(8,128)S(1)} %get-tuple-element.15), channel_id=1, source_target_pairs={{0,24},{8,16},{16,8},{24,0},{1,25},{9,17},{17,9},{25,1},{2,26},{10... | collective-permute-start | bytes 98312 | tf_op jit(solution)/shard_map/ppermute | solution.py:19
  5.2 4.8 %collective-permute-start.1 = (f32[64,128]{1,0:T(8,128)S(1)}, f32[64,128]{1,0:T(8,128)S(1)}, u32[]{:S(2)}, u32[]{:S(2)}) collective-permute-start(f32[64,128]{1,0:T(8,128)S(1)} %get-tuple-element.15), channel_id=1, source_target_pairs={{0,16},{8,24},{16,0},{24,8},{1,17},{9,25},{17,1},{25,9},{2,18},{10... | collective-permute-start | bytes 98312 | tf_op jit(solution)/shard_map/ppermute | solution.py:19
  6.6 3.9 %collective-permute-start.2 = (f32[64,128]{1,0:T(8,128)S(1)}, f32[64,128]{1,0:T(8,128)S(1)}, u32[]{:S(2)}, u32[]{:S(2)}) collective-permute-start(f32[64,128]{1,0:T(8,128)S(1)} %get-tuple-element.15), channel_id=1, source_target_pairs={{0,8},{8,0},{16,24},{24,16},{1,9},{9,1},{17,25},{25,17},{2,10},{10... | collective-permute-start | bytes 98312 | tf_op jit(solution)/shard_map/ppermute | solution.py:19
  6.7 3.8 %copy-start = (f32[3,4]{1,0:T(4,128)S(1)}, f32[3,4]{1,0:T(4,128)}, u32[]{:S(2)}) copy-start(f32[3,4]{1,0:T(4,128)} %coef_ref.3) | copy-start | bytes 148
  10.7 1.3 %collective-permute-start.3 = (f32[4,4,8,128]{3,2,1,0:T(8,128)S(1)}, f32[4,4,8,128]{3,2,1,0:T(8,128)S(1)}, u32[]{:S(2)}, u32[]{:S(2)}) collective-permute-start(f32[4,4,8,128]{3,2,1,0:T(8,128)S(1)} %get-tuple-element.24), channel_id=1, source_target_pairs={{0,1},{1,0},{2,3},{3,2},{4,5},{5,4},{6,7},{7,6},{8,9},{9,8},{10,11... | collective-permute-start | bytes 196616 | tf_op jit(solution)/shard_map/ppermute | solution.py:19
  12.1 4.7 %collective-permute-start.4 = (f32[4,8,128]{2,1,0:T(8,128)S(1)}, f32[4,8,128]{2,1,0:T(8,128)S(1)}, u32[]{:S(2)}, u32[]{:S(2)}) collective-permute-start(f32[4,8,128]{2,1,0:T(8,128)S(1)} %get-tuple-element.27), channel_id=1, source_target_pairs={{0,6},{1,7},{2,4},{3,5},{4,2},{5,3},{6,0},{7,1},{8,14},{9,15},{10,... | collective-permute-start | bytes 49160 | tf_op jit(solution)/shard_map/ppermute | solution.py:19
  14.6 3.7 %collective-permute-start.5 = (f32[4,8,128]{2,1,0:T(8,128)S(1)}, f32[4,8,128]{2,1,0:T(8,128)S(1)}, u32[]{:S(2)}, u32[]{:S(2)}) collective-permute-start(f32[4,8,128]{2,1,0:T(8,128)S(1)} %get-tuple-element.28), channel_id=1, source_target_pairs={{0,4},{1,5},{2,6},{3,7},{4,0},{5,1},{6,2},{7,3},{8,12},{9,13},{10,... | collective-permute-start | bytes 49160 | tf_op jit(solution)/shard_map/ppermute | solution.py:19
  15.1 3.7 %collective-permute-start.6 = (f32[4,8,128]{2,1,0:T(8,128)S(1)}, f32[4,8,128]{2,1,0:T(8,128)S(1)}, u32[]{:S(2)}, u32[]{:S(2)}) collective-permute-start(f32[4,8,128]{2,1,0:T(8,128)S(1)} %get-tuple-element.29), channel_id=1, source_target_pairs={{0,2},{1,3},{2,0},{3,1},{4,6},{5,7},{6,4},{7,5},{8,10},{9,11},{10,... | collective-permute-start | bytes 49160 | tf_op jit(solution)/shard_map/ppermute | solution.py:19

commit v8 on v6

--- a/solution.py
+++ b/solution.py
@@ -284,8 +284,8 @@
     view_parts = in_parts(-2.0 / (cells * view_count) * LOG2E)
     own_rows = planes // view_count
     chunk = 32
-    step_cells = 32
-    rows = 16
+    step_cells = 16
+    rows = 32
     lit_cells = 32
     whole = pl.BlockSpec(memory_space=VMEM)
     scalars = pl.BlockSpec(memory_space=pltpu.SMEM)

time: 19.6 us -> 19.6 us (level)
  no operation moved by 1% of the time
where the time goes in v8:
time: 19.6 us; the launch traced here: 19.5 us
  starting transfers between devices  8.29 us (42%)
  waiting for transfers between devices  5.69 us (29%)
  Pallas kernels  4.65 us (24%)
  other arithmetic  0.68 us (3%)
    ppermute x7, starting transfers between devices, swapped(): return lax.ppermute(x, axis, [(i, i ^ mask) for i in range(devices)])  8.29 us
    ppermute x7, waiting for transfers between devices, swapped(): return lax.ppermute(x, axis, [(i, i ^ mask) for i in range(devices)])  5.69 us
    pallas_call x1, Pallas kernels, body(): pl.pallas_call(functools.partial(local_kernel, rows, step_cells, in_parts...  2.31 us
    pallas_call x1, Pallas kernels, body(): pl.pallas_call(functools.partial(totals_kernel, chunk, light_count - 1),...  2.01 us
    add x1, other arithmetic, over(): total = total + piece[:3] * ahead[None]  0.61 us
  transfers between devices with their start and end apart: 7, of which 6 were waited for; matrix products, arithmetic and copies ran while one was open for 0% of the time, Pallas kernels for 13%

profile of v8, /device:TPU:0, one launch (start us, length us, event | category | flops | bytes accessed | tf_op | source)
XLA Modules:
  0.0 19.5 jit_solution(13717936590486225390)
XLA Ops:
  0.0 2.0 %totals_kernel.1 = (f32[64,128]{1,0:T(8,128)S(1)}, bf16[128,64,128]{2,1,0:T(8,128)(2,1)S(1)}) custom-call(s32[1]{0:T(128)} %bitcast.place_ref, bf16[128,64,128]{2,1,0:T(8,128)(2,1)} %density_ref.3), custom_call_target="tpu_custom_call" | custom-call | tf_op jit(solution)/shard_map/totals_kernel/pallas_call | solution.py:298
  2.0 3.1 %collective-permute-start = (f32[64,128]{1,0:T(8,128)S(1)}, f32[64,128]{1,0:T(8,128)S(1)}, u32[]{:S(2)}, u32[]{:S(2)}) collective-permute-start(f32[64,128]{1,0:T(8,128)S(1)} %get-tuple-element.16), channel_id=1, source_target_pairs={{0,24},{8,16},{16,8},{24,0},{1,25},{9,17},{17,9},{25,1},{2,26},{10... | collective-permute-start | bytes 98312 | tf_op jit(solution)/shard_map/ppermute | solution.py:19
  5.2 1.4 %collective-permute-start.1 = (f32[64,128]{1,0:T(8,128)S(1)}, f32[64,128]{1,0:T(8,128)S(1)}, u32[]{:S(2)}, u32[]{:S(2)}) collective-permute-start(f32[64,128]{1,0:T(8,128)S(1)} %get-tuple-element.16), channel_id=1, source_target_pairs={{0,16},{8,24},{16,0},{24,8},{1,17},{9,25},{17,1},{25,9},{2,18},{10... | collective-permute-start | bytes 98312 | tf_op jit(solution)/shard_map/ppermute | solution.py:19
  6.6 0.1 collective-permute-start.2
  6.7 0.0 copy-start
  6.7 2.3 %local_kernel.1 = (f32[128,64,128]{2,1,0:T(8,128)S(1)}, f32[128,64,128]{2,1,0:T(8,128)S(1)}, f32[5,64,128]{2,1,0:T(8,128)S(1)}) custom-call(s32[1]{0:T(128)} %bitcast.place_ref, bf16[128,64,128]{2,1,0:T(8,128)(2,1)S(1)} %brick_kernel.1.brick_ref), custom_call_target="tpu_custom_call" | custom-call | flops 20971520 | bytes 8388608 | tf_op jit(solution)/shard_map/local_kernel/pallas_call | solution.py:325
  9.1 0.0 collective-permute-done
  9.1 0.9 %collective-permute-done.1 = f32[64,128]{1,0:T(8,128)S(1)} collective-permute-done((f32[64,128]{1,0:T(8,128)S(1)}, f32[64,128]{1,0:T(8,128)S(1)}, u32[]{:S(2)}, u32[]{:S(2)}) %collective-permute-start.1) | collective-permute-done | bytes 32800 | tf_op jit(solution)/shard_map/ppermute | solution.py:19
  10.0 0.5 %collective-permute-done.2 = f32[64,128]{1,0:T(8,128)S(1)} collective-permute-done((f32[64,128]{1,0:T(8,128)S(1)}, f32[64,128]{1,0:T(8,128)S(1)}, u32[]{:S(2)}, u32[]{:S(2)}) %collective-permute-start.2) | collective-permute-done | bytes 32800 | tf_op jit(solution)/shard_map/ppermute | solution.py:19
  10.5 0.0 copy-done
  10.5 0.2 lit_kernel.2
  10.7 0.1 collective-permute-start.3
  10.8 0.1 lit_kernel.3
  10.9 1.1 %collective-permute-done.3 = f32[4,4,8,128]{3,2,1,0:T(8,128)S(1)} collective-permute-done((f32[4,4,8,128]{3,2,1,0:T(8,128)S(1)}, f32[4,4,8,128]{3,2,1,0:T(8,128)S(1)}, u32[]{:S(2)}, u32[]{:S(2)}) %collective-permute-start.3) | collective-permute-done | bytes 65568 | tf_op jit(solution)/shard_map/ppermute | solution.py:19
  12.1 2.5 %collective-permute-start.4 = (f32[4,8,128]{2,1,0:T(8,128)S(1)}, f32[4,8,128]{2,1,0:T(8,128)S(1)}, u32[]{:S(2)}, u32[]{:S(2)}) collective-permute-start(f32[4,8,128]{2,1,0:T(8,128)S(1)} %get-tuple-element.29), channel_id=1, source_target_pairs={{0,6},{1,7},{2,4},{3,5},{4,2},{5,3},{6,0},{7,1},{8,14},{9,15},{10,... | collective-permute-start | bytes 49160 | tf_op jit(solution)/shard_map/ppermute | solution.py:19
  14.6 0.5 %collective-permute-start.5 = (f32[4,8,128]{2,1,0:T(8,128)S(1)}, f32[4,8,128]{2,1,0:T(8,128)S(1)}, u32[]{:S(2)}, u32[]{:S(2)}) collective-permute-start(f32[4,8,128]{2,1,0:T(8,128)S(1)} %get-tuple-element.30), channel_id=1, source_target_pairs={{0,4},{1,5},{2,6},{3,7},{4,0},{5,1},{6,2},{7,3},{8,12},{9,13},{10,... | collective-permute-start | bytes 49160 | tf_op jit(solution)/shard_map/ppermute | solution.py:19
  15.1 0.5 %collective-permute-start.6 = (f32[4,8,128]{2,1,0:T(8,128)S(1)}, f32[4,8,128]{2,1,0:T(8,128)S(1)}, u32[]{:S(2)}, u32[]{:S(2)}) collective-permute-start(f32[4,8,128]{2,1,0:T(8,128)S(1)} %get-tuple-element.31), channel_id=1, source_target_pairs={{0,2},{1,3},{2,0},{3,1},{4,6},{5,7},{6,4},{7,5},{8,10},{9,11},{10,... | collective-permute-start | bytes 49160 | tf_op jit(solution)/shard_map/ppermute | solution.py:19
  15.6 1.1 %collective-permute-done.4 = f32[4,8,128]{2,1,0:T(8,128)S(1)} collective-permute-done((f32[4,8,128]{2,1,0:T(8,128)S(1)}, f32[4,8,128]{2,1,0:T(8,128)S(1)}, u32[]{:S(2)}, u32[]{:S(2)}) %collective-permute-start.4) | collective-permute-done | bytes 16416 | tf_op jit(solution)/shard_map/ppermute | solution.py:19
  16.8 1.5 %collective-permute-done.5 = f32[4,8,128]{2,1,0:T(8,128)S(1)} collective-permute-done((f32[4,8,128]{2,1,0:T(8,128)S(1)}, f32[4,8,128]{2,1,0:T(8,128)S(1)}, u32[]{:S(2)}, u32[]{:S(2)}) %collective-permute-start.5) | collective-permute-done | bytes 16416 | tf_op jit(solution)/shard_map/ppermute | solution.py:19
  18.3 0.5 %collective-permute-done.6 = f32[4,8,128]{2,1,0:T(8,128)S(1)} collective-permute-done((f32[4,8,128]{2,1,0:T(8,128)S(1)}, f32[4,8,128]{2,1,0:T(8,128)S(1)}, u32[]{:S(2)}, u32[]{:S(2)}) %collective-permute-start.6) | collective-permute-done | bytes 16416 | tf_op jit(solution)/shard_map/ppermute | solution.py:19
  18.8 0.6 %fusion.5 = f32[3,8,128]{2,1,0:T(8,128)} fusion(f32[4,3,8,128]{3,2,1,0:T(8,128)S(1)} %fusion.2, f32[4,8,128]{2,1,0:T(8,128)S(1)} %collective-permute-done.6, f32[4,8,128]{2,1,0:T(8,128)S(1)} %collective-permute-done.5, f32[4,8,128]{2,1,0:T(8,128)S(1)} %collective-permute-done.4, f32[8,128]{1,0:T(8,128)S(1)} %get-tuple-element.35, f32[8,128]{1,0:T(8,128)S(1)} %fusion.8, ...), kind=kLoop, calls=%fused_computation.15 | loop fusion | flops 21504 | bytes 77824 | tf_op jit(solution)/shard_map/add | solution.py:275
  (9 shorter events, 0.1 us)
Async XLA Ops:
  2.0 7.1 %collective-permute-start = (f32[64,128]{1,0:T(8,128)S(1)}, f32[64,128]{1,0:T(8,128)S(1)}, u32[]{:S(2)}, u32[]{:S(2)}) collective-permute-start(f32[64,128]{1,0:T(8,128)S(1)} %get-tuple-element.16), channel_id=1, source_target_pairs={{0,24},{8,16},{16,8},{24,0},{1,25},{9,17},{17,9},{25,1},{2,26},{10... | collective-permute-start | bytes 98312 | tf_op jit(solution)/shard_map/ppermute | solution.py:19
  5.2 4.8 %collective-permute-start.1 = (f32[64,128]{1,0:T(8,128)S(1)}, f32[64,128]{1,0:T(8,128)S(1)}, u32[]{:S(2)}, u32[]{:S(2)}) collective-permute-start(f32[64,128]{1,0:T(8,128)S(1)} %get-tuple-element.16), channel_id=1, source_target_pairs={{0,16},{8,24},{16,0},{24,8},{1,17},{9,25},{17,1},{25,9},{2,18},{10... | collective-permute-start | bytes 98312 | tf_op jit(solution)/shard_map/ppermute | solution.py:19
  6.6 3.9 %collective-permute-start.2 = (f32[64,128]{1,0:T(8,128)S(1)}, f32[64,128]{1,0:T(8,128)S(1)}, u32[]{:S(2)}, u32[]{:S(2)}) collective-permute-start(f32[64,128]{1,0:T(8,128)S(1)} %get-tuple-element.16), channel_id=1, source_target_pairs={{0,8},{8,0},{16,24},{24,16},{1,9},{9,1},{17,25},{25,17},{2,10},{10... | collective-permute-start | bytes 98312 | tf_op jit(solution)/shard_map/ppermute | solution.py:19
  6.7 3.8 %copy-start = (f32[3,4]{1,0:T(4,128)S(1)}, f32[3,4]{1,0:T(4,128)}, u32[]{:S(2)}) copy-start(f32[3,4]{1,0:T(4,128)} %coef_ref.3) | copy-start | bytes 148
  10.7 1.3 %collective-permute-start.3 = (f32[4,4,8,128]{3,2,1,0:T(8,128)S(1)}, f32[4,4,8,128]{3,2,1,0:T(8,128)S(1)}, u32[]{:S(2)}, u32[]{:S(2)}) collective-permute-start(f32[4,4,8,128]{3,2,1,0:T(8,128)S(1)} %pad_maximum_fusion.1), channel_id=1, source_target_pairs={{0,1},{1,0},{2,3},{3,2},{4,5},{5,4},{6,7},{7,6},{8,9},{9,8},{10,11... | collective-permute-start | bytes 196616 | tf_op jit(solution)/shard_map/ppermute | solution.py:19
  12.1 4.7 %collective-permute-start.4 = (f32[4,8,128]{2,1,0:T(8,128)S(1)}, f32[4,8,128]{2,1,0:T(8,128)S(1)}, u32[]{:S(2)}, u32[]{:S(2)}) collective-permute-start(f32[4,8,128]{2,1,0:T(8,128)S(1)} %get-tuple-element.29), channel_id=1, source_target_pairs={{0,6},{1,7},{2,4},{3,5},{4,2},{5,3},{6,0},{7,1},{8,14},{9,15},{10,... | collective-permute-start | bytes 49160 | tf_op jit(solution)/shard_map/ppermute | solution.py:19
  14.6 3.7 %collective-permute-start.5 = (f32[4,8,128]{2,1,0:T(8,128)S(1)}, f32[4,8,128]{2,1,0:T(8,128)S(1)}, u32[]{:S(2)}, u32[]{:S(2)}) collective-permute-start(f32[4,8,128]{2,1,0:T(8,128)S(1)} %get-tuple-element.30), channel_id=1, source_target_pairs={{0,4},{1,5},{2,6},{3,7},{4,0},{5,1},{6,2},{7,3},{8,12},{9,13},{10,... | collective-permute-start | bytes 49160 | tf_op jit(solution)/shard_map/ppermute | solution.py:19
  15.1 3.7 %collective-permute-start.6 = (f32[4,8,128]{2,1,0:T(8,128)S(1)}, f32[4,8,128]{2,1,0:T(8,128)S(1)}, u32[]{:S(2)}, u32[]{:S(2)}) collective-permute-start(f32[4,8,128]{2,1,0:T(8,128)S(1)} %get-tuple-element.31), channel_id=1, source_target_pairs={{0,2},{1,3},{2,0},{3,1},{4,6},{5,7},{6,4},{7,5},{8,10},{9,11},{10,... | collective-permute-start | bytes 49160 | tf_op jit(solution)/shard_map/ppermute | solution.py:19
